TPU v7x, 128 devices: a whole 4x4x4 slice. The times are simulated.
128 devices in a mesh: section: 2 (over y_hi), tensor: 2 (over core), dp: 32 (over z, x, y_lo).
Axes of the slice: x: 4, y: 4 (y_hi: 2, y_lo: 2; y = y_hi * 2 + y_lo), z: 4, core: 2. Of those that a mesh axis runs over, the one named last changes fastest.
Arguments:
- images: bfloat16 [32, 2, 1, 197, 1024], P('dp'), may hold values from -6 to 6
- cotangent: bfloat16 [32, 2, 1, 197, 1024], P('dp'), may hold values from -6 to 6
- shard_count: int32 [32], P('dp'), may hold values from 1 to 2, 48 in all
- slot_order: int32 [32, 2], P('dp'), may hold values from 0 to 1, each once within a row
- attend_gain: float32 [2, 1024], P('section'), may hold values from 0.5 to 1.5
- attend_input: bfloat16 [2, 1024, 3, 1024], P('section', None, None, 'tensor'), may hold values from -0.1875 to 0.1875
- attend_output: bfloat16 [2, 1024, 1024], P('section', 'tensor'), may hold values from -1.25 to 1.25
- feed_gain: float32 [2, 1024], P('section'), may hold values from 0.5 to 1.5
- feed_expand: bfloat16 [2, 1024, 4096], P('section', None, 'tensor'), may hold values from -0.1875 to 0.1875
- feed_reduce: bfloat16 [2, 4096, 1024], P('section', 'tensor'), may hold values from -0.09375 to 0.09375
Outputs:
- block_outputs: bfloat16 [2, 32, 2, 1, 197, 1024], P('section', 'dp')
- input_gradient: bfloat16 [2, 32, 2, 1, 197, 1024], P('section', 'dp')
- attend_gain_gradient: float32 [2, 1024], P('section', 'dp')
- attend_input_gradient: float32 [2, 1024, 3, 1024], P('section', 'dp', None, 'tensor')
- attend_output_gradient: float32 [2, 1024, 1024], P('section', ('tensor', 'dp'))
- feed_gain_gradient: float32 [2, 1024], P('section', 'dp')
- feed_expand_gradient: float32 [2, 1024, 4096], P('section', 'dp', 'tensor')
- feed_reduce_gradient: float32 [2, 4096, 1024], P('section', ('tensor', 'dp'))
Inputs may be any that keep to these rules, and one draw needn't show every extreme that they name: `shard_count`: the counts sum to 48, and 16 shards hold 2 images. `slot_order`: each row is a permutation; its first shard_count entries name the slots that hold images.
All inputs are finite; a program needn't handle non-finite values.
Results may differ from a plain program's by a relative error of at most 0.03.
Values may be sent and summed in bfloat16 or wider, within the bound.
A program may use at most 128 MiB of HBM per device.

v0:
```python
import jax
import jax.numpy as jnp
from jax import lax
from jax.sharding import PartitionSpec as P

HEAD_DIM = 64


epsilon = 1e-06
score_scale = 0.125


def shifted(value, axis, steps):
    count = lax.axis_size(axis)
    first, last = (max(0, -steps), min(count, count - steps))
    return lax.ppermute(value, axis, [(source, source + steps) for source in range(first, last)])


def layer_norm(values, gain):
    centre = values - jnp.mean(values, axis=-1, keepdims=True)
    scale_inv = lax.rsqrt(jnp.mean(centre * centre, axis=-1, keepdims=True) + epsilon)
    normed = centre * scale_inv
    return (normed * gain, normed, scale_inv)


def norm_back(upstream, normed, scale_inv, gain):
    scaled = upstream * gain
    centred = scaled - jnp.mean(scaled, axis=-1, keepdims=True)
    return scale_inv * (centred - normed * jnp.mean(scaled * normed, axis=-1, keepdims=True))


def gelu_exact(values):
    return jax.nn.gelu(values, approximate=False)


def split_heads(projected):
    parts, image_count, token_count, local_width = projected.shape
    return projected.reshape(parts, image_count, token_count, local_width // HEAD_DIM, HEAD_DIM)


def forward_block(
    inputs, attend_gain, attend_input, attend_output, feed_gain, feed_expand, feed_reduce
):
    image_count, token_count, model_width = inputs.shape
    residual = inputs.astype(jnp.float32)
    normed_one, hat_one, inverse_one = layer_norm(residual, attend_gain)
    norm_one = normed_one.astype(jnp.bfloat16)
    projected = jnp.einsum(
        "cld,dje->jcle", norm_one, attend_input, preferred_element_type=jnp.float32
    ).astype(jnp.bfloat16)
    heads_view = split_heads(projected)
    scores = (
        jnp.einsum(
            "cqhe,ckhe->chqk", heads_view[0], heads_view[1], preferred_element_type=jnp.float32
        )
        * score_scale
    )
    row_max = jnp.max(scores, axis=-1, keepdims=True)
    row_total = jnp.sum(jnp.exp(scores - row_max), axis=-1, keepdims=True)
    log_total = row_max + jnp.log(row_total)
    softmax_low = jnp.exp(scores - log_total).astype(jnp.bfloat16)
    mixed_heads = jnp.einsum(
        "chqk,ckhe->cqhe", softmax_low, heads_view[2], preferred_element_type=jnp.float32
    ).astype(jnp.bfloat16)
    mixed_rows = mixed_heads.reshape(image_count, token_count, projected.shape[3])
    attend_terms = jnp.einsum(
        "cle,ed->cld", mixed_rows, attend_output, preferred_element_type=jnp.float32
    )
    attend_sum = lax.psum(attend_terms.astype(jnp.bfloat16), "tensor").astype(jnp.float32)
    middle = residual + attend_sum
    normed_two, hat_two, inverse_two = layer_norm(middle, feed_gain)
    norm_two = normed_two.astype(jnp.bfloat16)
    expanded = jnp.einsum("cld,df->clf", norm_two, feed_expand, preferred_element_type=jnp.float32)
    activated = gelu_exact(expanded).astype(jnp.bfloat16)
    feed_terms = jnp.einsum(
        "clf,fd->cld", activated, feed_reduce, preferred_element_type=jnp.float32
    )
    feed_sum = lax.psum(feed_terms.astype(jnp.bfloat16), "tensor").astype(jnp.float32)
    saved_state = (
        hat_one,
        inverse_one,
        norm_one,
        projected,
        log_total,
        mixed_rows,
        hat_two,
        inverse_two,
        norm_two,
        expanded,
        activated,
    )
    return (middle + feed_sum, saved_state)


def backward_block(
    incoming,
    saved_state,
    attend_gain,
    attend_input,
    attend_output,
    feed_gain,
    feed_expand,
    feed_reduce,
):
    (
        hat_one,
        inverse_one,
        norm_one,
        projected,
        log_total,
        mixed_rows,
        hat_two,
        inverse_two,
        norm_two,
        expanded,
        activated,
    ) = saved_state
    reduce_gradient = incoming.astype(jnp.bfloat16)
    reduce_weight_gradient = jnp.einsum(
        "clf,cld->fd", activated, reduce_gradient, preferred_element_type=jnp.float32
    )
    activated_gradient = jnp.einsum(
        "cld,fd->clf", reduce_gradient, feed_reduce, preferred_element_type=jnp.float32
    )
    unused_value, gelu_pullback = jax.vjp(gelu_exact, expanded)
    expand_gradient = gelu_pullback(activated_gradient)[0].astype(jnp.bfloat16)
    expand_weight_gradient = jnp.einsum(
        "cld,clf->df", norm_two, expand_gradient, preferred_element_type=jnp.float32
    )
    norm_two_terms = jnp.einsum(
        "clf,df->cld", expand_gradient, feed_expand, preferred_element_type=jnp.float32
    )
    norm_two_gradient = lax.psum(norm_two_terms.astype(jnp.bfloat16), "tensor").astype(jnp.float32)
    feed_gain_part = jnp.sum(norm_two_gradient * hat_two, axis=(0, 1))
    middle_gradient = incoming + norm_back(norm_two_gradient, hat_two, inverse_two, feed_gain)
    middle_low = middle_gradient.astype(jnp.bfloat16)
    output_weight_gradient = jnp.einsum(
        "cle,cld->ed", mixed_rows, middle_low, preferred_element_type=jnp.float32
    )
    mixed_gradient = jnp.einsum(
        "cld,ed->cle", middle_low, attend_output, preferred_element_type=jnp.float32
    ).astype(jnp.bfloat16)
    heads_view = split_heads(projected)
    query_rows, key_rows, value_rows = (heads_view[0], heads_view[1], heads_view[2])
    mixed_split = mixed_gradient.reshape(query_rows.shape)
    scores = (
        jnp.einsum("cqhe,ckhe->chqk", query_rows, key_rows, preferred_element_type=jnp.float32)
        * score_scale
    )
    softmax_full = jnp.exp(scores - log_total)
    softmax_low = softmax_full.astype(jnp.bfloat16)
    value_gradient = jnp.einsum(
        "chqk,cqhe->ckhe", softmax_low, mixed_split, preferred_element_type=jnp.float32
    )
    softmax_gradient = jnp.einsum(
        "cqhe,ckhe->chqk", mixed_split, value_rows, preferred_element_type=jnp.float32
    )
    row_inner = jnp.sum(softmax_gradient * softmax_full, axis=-1, keepdims=True)
    scores_gradient = (softmax_full * (softmax_gradient - row_inner)).astype(jnp.bfloat16)
    query_gradient = (
        jnp.einsum("chqk,ckhe->cqhe", scores_gradient, key_rows, preferred_element_type=jnp.float32)
        * score_scale
    )
    key_gradient = (
        jnp.einsum(
            "chqk,cqhe->ckhe", scores_gradient, query_rows, preferred_element_type=jnp.float32
        )
        * score_scale
    )
    projected_gradient = (
        jnp.stack([query_gradient, key_gradient, value_gradient])
        .astype(jnp.bfloat16)
        .reshape(projected.shape)
    )
    input_weight_gradient = jnp.einsum(
        "cld,jcle->dje", norm_one, projected_gradient, preferred_element_type=jnp.float32
    )
    norm_one_terms = jnp.einsum(
        "jcle,dje->cld", projected_gradient, attend_input, preferred_element_type=jnp.float32
    )
    norm_one_gradient = lax.psum(norm_one_terms.astype(jnp.bfloat16), "tensor").astype(jnp.float32)
    attend_gain_part = jnp.sum(norm_one_gradient * hat_one, axis=(0, 1))
    entry_gradient = middle_gradient + norm_back(
        norm_one_gradient, hat_one, inverse_one, attend_gain
    )
    weight_terms = (
        attend_gain_part,
        input_weight_gradient,
        output_weight_gradient,
        feed_gain_part,
        expand_weight_gradient,
        reduce_weight_gradient,
    )
    return (entry_gradient, weight_terms)


def per_device(
    images,
    cotangent,
    shard_count,
    slot_order,
    attend_gain,
    attend_input,
    attend_output,
    feed_gain,
    feed_expand,
    feed_reduce,
):
    batches = images.shape[1]
    slot_width = images.shape[2]
    weights = (
        attend_gain[0],
        attend_input[0],
        attend_output[0],
        feed_gain[0],
        feed_expand[0],
        feed_reduce[0],
    )
    slot_numbers = jnp.arange(batches * slot_width, dtype=jnp.int32)
    matches = slot_order[0][:, None] == slot_numbers[None, :]
    taken_rows = (slot_numbers < shard_count[0])[:, None]
    live_slots = (
        jnp.sum(jnp.where(matches & taken_rows, 1.0, 0.0), axis=0)
        .astype(jnp.float32)
        .reshape(batches, slot_width)
    )
    first_section = lax.axis_index("section") == 0
    empty_block = jnp.zeros(images.shape[2:], jnp.bfloat16)
    received = empty_block
    produced = []
    saved_states = []
    for forward_tick in range(batches + 1):
        own_input = images[0, forward_tick] if forward_tick < batches else empty_block
        inputs = jnp.where(first_section, own_input, received)
        result, saved_state = forward_block(inputs, *weights)
        result_low = result.astype(jnp.bfloat16)
        produced.append(result_low)
        saved_states.append(saved_state)
        if forward_tick < batches:
            received = shifted(result_low, "section", 1)
    arriving = empty_block
    returned = []
    totals = None
    for backward_tick in range(batches + 1):
        saved_index = batches - backward_tick
        if backward_tick < batches:
            batch_slot = batches - 1 - backward_tick
            last_gradient = (
                cotangent[0, batch_slot].astype(jnp.float32) * live_slots[batch_slot][:, None, None]
            )
        else:
            last_gradient = jnp.zeros(images.shape[2:], jnp.float32)
        incoming = jnp.where(first_section, arriving.astype(jnp.float32), last_gradient)
        entry_gradient, tick_terms = backward_block(incoming, saved_states[saved_index], *weights)
        entry_low = entry_gradient.astype(jnp.bfloat16)
        returned.append(entry_low)
        totals = tick_terms if totals is None else jax.tree.map(jnp.add, totals, tick_terms)
        if backward_tick < batches:
            arriving = shifted(entry_low, "section", -1)
    total_gain_one, total_input, total_output, total_gain_two, total_expand, total_reduce = totals
    totals = (
        lax.psum_scatter(
            total_gain_one.astype(jnp.bfloat16), "dp", scatter_dimension=0, tiled=True
        ).astype(jnp.float32),
        lax.psum_scatter(
            total_input.astype(jnp.bfloat16), "dp", scatter_dimension=0, tiled=True
        ).astype(jnp.float32),
        lax.psum_scatter(
            total_output.astype(jnp.bfloat16), "dp", scatter_dimension=0, tiled=True
        ).astype(jnp.float32),
        lax.psum_scatter(
            total_gain_two.astype(jnp.bfloat16), "dp", scatter_dimension=0, tiled=True
        ).astype(jnp.float32),
        lax.psum_scatter(
            total_expand.astype(jnp.bfloat16), "dp", scatter_dimension=0, tiled=True
        ).astype(jnp.float32),
        lax.psum_scatter(
            total_reduce.astype(jnp.bfloat16), "dp", scatter_dimension=0, tiled=True
        ).astype(jnp.float32),
    )
    block_outputs = jnp.stack(
        [
            jnp.where(first_section, produced[batch_index], produced[batch_index + 1])
            for batch_index in range(batches)
        ]
    )
    input_gradient = jnp.stack(
        [
            jnp.where(
                first_section, returned[batches - batch_index], returned[batches - 1 - batch_index]
            )
            for batch_index in range(batches)
        ]
    )
    return (
        block_outputs[None, None],
        input_gradient[None, None],
        totals[0][None],
        totals[1][None],
        totals[2][None],
        totals[3][None],
        totals[4][None],
        totals[5][None],
    )


def solution(mesh):
    in_specs = (
        P("dp", None, None, None, None),
        P("dp", None, None, None, None),
        P("dp"),
        P("dp", None),
        P("section", None),
        P("section", None, None, "tensor"),
        P("section", "tensor", None),
        P("section", None),
        P("section", None, "tensor"),
        P("section", "tensor", None),
    )
    out_specs = (
        P("section", "dp", None, None, None, None),
        P("section", "dp", None, None, None, None),
        P("section", "dp"),
        P("section", "dp", None, "tensor"),
        P("section", ("tensor", "dp"), None),
        P("section", "dp"),
        P("section", "dp", "tensor"),
        P("section", ("tensor", "dp"), None),
    )
    return jax.shard_map(
        per_device, mesh=mesh, in_specs=in_specs, out_specs=out_specs, check_vma=False
    )
```

profile of v0, /device:TPU:0, one launch (start us, length us, event | category | flops | bytes accessed | tf_op | source)
XLA Modules:
  0.0 1206.4 jit_solution(1499390911603414484)
XLA Ops:
  25.4 26.7 %all-reduce.16.cloned.1.call-done = bf16[1,197,1024]{2,1,0:T(8,128)(2,1)} async-done(((bf16[1,197,1024]{2,1,0:T(8,128)(2,1)}), bf16[1,197,1024]{2,1,0:T(8,128)(2,1)}) %all-reduce.16.cloned.1.call-update) | async-done | bytes 403472 | tf_op jit(solution)/shard_map/psum | solution.py:69
  54.6 8.4 multiply_convert_fusion.5
  65.8 25.6 %all-reduce.18.cloned.1.call-done = bf16[1,197,1024]{2,1,0:T(8,128)(2,1)} async-done(((bf16[1,197,1024]{2,1,0:T(8,128)(2,1)}), bf16[1,197,1024]{2,1,0:T(8,128)(2,1)}) %all-reduce.18.cloned.1.call-update) | async-done | bytes 403472 | tf_op jit(solution)/shard_map/psum | solution.py:78
  92.8 5.5 collective-permute-start
  98.3 8.7 collective-permute-done
  119.3 26.4 %all-reduce.20.cloned.1.call-done = bf16[1,197,1024]{2,1,0:T(8,128)(2,1)} async-done(((bf16[1,197,1024]{2,1,0:T(8,128)(2,1)}), bf16[1,197,1024]{2,1,0:T(8,128)(2,1)}) %all-reduce.20.cloned.1.call-update) | async-done | bytes 403472 | tf_op jit(solution)/shard_map/psum | solution.py:69
  148.3 8.4 multiply_convert_fusion.4
  159.5 25.6 %all-reduce.22.cloned.1.call-done = bf16[1,197,1024]{2,1,0:T(8,128)(2,1)} async-done(((bf16[1,197,1024]{2,1,0:T(8,128)(2,1)}), bf16[1,197,1024]{2,1,0:T(8,128)(2,1)}) %all-reduce.22.cloned.1.call-update) | async-done | bytes 403472 | tf_op jit(solution)/shard_map/psum | solution.py:78
  193.6 7.9 collective-permute-done.1
  219.1 21.0 %all-reduce.24.cloned.1.call-done = bf16[1,197,1024]{2,1,0:T(8,128)(2,1)} async-done(((bf16[1,197,1024]{2,1,0:T(8,128)(2,1)}), bf16[1,197,1024]{2,1,0:T(8,128)(2,1)}) %all-reduce.24.cloned.1.call-update) | async-done | bytes 403472 | tf_op jit(solution)/shard_map/psum | solution.py:69
  242.7 7.7 multiply_convert_fusion.3
  256.6 25.6 %all-reduce.26.cloned.1.call-done = bf16[1,197,1024]{2,1,0:T(8,128)(2,1)} async-done(((bf16[1,197,1024]{2,1,0:T(8,128)(2,1)}), bf16[1,197,1024]{2,1,0:T(8,128)(2,1)}) %all-reduce.26.cloned.1.call-update) | async-done | bytes 403472 | tf_op jit(solution)/shard_map/psum | solution.py:133
  305.4 25.8 %all-reduce.28.cloned.1.call-done = bf16[1,197,1024]{2,1,0:T(8,128)(2,1)} async-done(((bf16[1,197,1024]{2,1,0:T(8,128)(2,1)}), bf16[1,197,1024]{2,1,0:T(8,128)(2,1)}) %all-reduce.28.cloned.1.call-update) | async-done | bytes 403472 | tf_op jit(solution)/shard_map/psum | solution.py:181
  337.1 13.8 %collective-permute-done.2 = bf16[1,197,1024]{2,1,0:T(8,128)(2,1)S(1)} collective-permute-done((bf16[1,197,1024]{2,1,0:T(8,128)(2,1)S(1)}, bf16[1,197,1024]{2,1,0:T(8,128)(2,1)S(1)}, u32[]{:S(2)}, u32[]{:S(2)}) %collective-permute-start.2) | collective-permute-done | bytes 403488 | tf_op jit(solution)/shard_map/ppermute | solution.py:16
  350.9 5.7 add_convert_fusion.5
  360.1 23.8 %all-reduce.30.cloned.1.call-done = bf16[1,197,1024]{2,1,0:T(8,128)(2,1)} async-done(((bf16[1,197,1024]{2,1,0:T(8,128)(2,1)}), bf16[1,197,1024]{2,1,0:T(8,128)(2,1)}) %all-reduce.30.cloned.1.call-update) | async-done | bytes 403472 | tf_op jit(solution)/shard_map/psum | solution.py:133
  407.4 25.5 %all-reduce.32.cloned.1.call-done = bf16[1,197,1024]{2,1,0:T(8,128)(2,1)} async-done(((bf16[1,197,1024]{2,1,0:T(8,128)(2,1)}), bf16[1,197,1024]{2,1,0:T(8,128)(2,1)}) %all-reduce.32.cloned.1.call-update) | async-done | bytes 403472 | tf_op jit(solution)/shard_map/psum | solution.py:181
  439.8 13.8 %collective-permute-done.3 = bf16[1,197,1024]{2,1,0:T(8,128)(2,1)S(1)} collective-permute-done((bf16[1,197,1024]{2,1,0:T(8,128)(2,1)S(1)}, bf16[1,197,1024]{2,1,0:T(8,128)(2,1)S(1)}, u32[]{:S(2)}, u32[]{:S(2)}) %collective-permute-start.3) | collective-permute-done | bytes 403488 | tf_op jit(solution)/shard_map/ppermute | solution.py:16
  465.9 19.3 %all-reduce.34.cloned.1.call-done = bf16[1,197,1024]{2,1,0:T(8,128)(2,1)} async-done(((bf16[1,197,1024]{2,1,0:T(8,128)(2,1)}), bf16[1,197,1024]{2,1,0:T(8,128)(2,1)}) %all-reduce.34.cloned.1.call-update) | async-done | bytes 403472 | tf_op jit(solution)/shard_map/psum | solution.py:133
  546.4 83.1 %all-reduce.2 = (bf16[1024]{0:T(1024)(128)(2,1)S(1)}, bf16[1024]{0:T(1024)(128)(2,1)S(1)}) all-reduce(bf16[1024]{0:T(1024)(128)(2,1)S(1)} %add_convert_fusion.11, bf16[1024]{0:T(1024)(128)(2,1)S(1)} %copy-done.122), channel_id=2, replica_groups=mesh['section'=2,'tensor'=2,'dp'=32] {'dp'}, use_global_device_ids=true, to_apply=%region_49.50.clone | all-reduce | flops 2048 | bytes 8192
  630.7 68.3 %reduce-scatter.7.cloned.1.call-done = bf16[16,1024]{1,0:T(8,128)(2,1)} async-done(((bf16[512,1024]{1,0:T(8,128)(2,1)}), bf16[16,1024]{1,0:T(8,128)(2,1)}) %reduce-scatter.7.cloned.1.call-update) | async-done | bytes 32784 | tf_op jit(solution)/shard_map/reduce_scatter | solution.py:268
  700.4 163.0 %reduce-scatter.5.cloned.1.call-done = bf16[32,3,512]{2,0,1:T(8,128)(2,1)} async-done(((bf16[1024,3,512]{2,0,1:T(8,128)(2,1)}), bf16[32,3,512]{2,0,1:T(8,128)(2,1)}) %reduce-scatter.5.cloned.1.call-update) | async-done | bytes 98320 | tf_op jit(solution)/shard_map/reduce_scatter | solution.py:265
  865.0 166.2 %reduce-scatter.9.cloned.1.call-done = bf16[32,2048]{1,0:T(8,128)(2,1)} async-done(((bf16[1024,2048]{1,0:T(8,128)(2,1)}), bf16[32,2048]{1,0:T(8,128)(2,1)}) %reduce-scatter.9.cloned.1.call-update) | async-done | bytes 131088 | tf_op jit(solution)/shard_map/reduce_scatter | solution.py:274
  1032.8 165.3 %reduce-scatter.11.cloned.1.call-done = bf16[64,1024]{1,0:T(8,128)(2,1)} async-done(((bf16[2048,1024]{1,0:T(8,128)(2,1)}), bf16[64,1024]{1,0:T(8,128)(2,1)}) %reduce-scatter.11.cloned.1.call-update) | async-done | bytes 131088 | tf_op jit(solution)/shard_map/reduce_scatter | solution.py:277
  (451 shorter events, 218.5 us)
Async XLA Ops:
  7.2 44.9 %all-reduce.16.cloned.1.call-start = ((), (), s32[]{:S(2)}) async-start(), calls=%async_computation.4 | async-start | bytes 819200 | tf_op jit(solution)/shard_map/psum | solution.py:69
  12.7 78.7 %copy-start.10 = (bf16[1,1,1,197,1024]{4,3,2,1,0:T(8,128)(2,1)}, bf16[1,1,1,197,1024]{4,3,2,1,0:T(8,128)(2,1)S(1)}, u32[]{:S(2)}) copy-start(bf16[1,1,1,197,1024]{4,3,2,1,0:T(8,128)(2,1)S(1)} %get-tuple-element.75) | copy-start | bytes 1210372
  25.3 66.0 %all-reduce.18.cloned.1.call-start = ((), (), s32[]{:S(2)}) async-start(), calls=%async_computation.5 | async-start | bytes 819200 | tf_op jit(solution)/shard_map/psum | solution.py:78
  65.8 79.9 %all-reduce.20.cloned.1.call-start = ((), (), s32[]{:S(2)}) async-start(), calls=%async_computation.6 | async-start | bytes 819200 | tf_op jit(solution)/shard_map/psum | solution.py:69
  92.8 14.2 %collective-permute-start = (bf16[1,197,1024]{2,1,0:T(8,128)(2,1)S(1)}, bf16[1,197,1024]{2,1,0:T(8,128)(2,1)S(1)}, u32[]{:S(2)}, u32[]{:S(2)}) collective-permute-start(bf16[1,197,1024]{2,1,0:T(8,128)(2,1)S(1)} %add_convert_fusion.9), channel_id=1, source_target_pairs={{0,64},{1,65},{2,66},{3,67},{4,68},{5,69},{6,70},{7,71},{8,72},{9,... | collective-permute-start | bytes 1210376 | tf_op jit(solution)/shard_map/ppermute | solution.py:16
  119.2 65.8 %all-reduce.22.cloned.1.call-start = ((), (), s32[]{:S(2)}) async-start(), calls=%async_computation.7 | async-start | bytes 819200 | tf_op jit(solution)/shard_map/psum | solution.py:78
  159.5 80.6 %all-reduce.24.cloned.1.call-start = ((), (), s32[]{:S(2)}) async-start(), calls=%async_computation.8 | async-start | bytes 819200 | tf_op jit(solution)/shard_map/psum | solution.py:69
  187.4 14.1 %collective-permute-start.1 = (bf16[1,197,1024]{2,1,0:T(8,128)(2,1)S(1)}, bf16[1,197,1024]{2,1,0:T(8,128)(2,1)S(1)}, u32[]{:S(2)}, u32[]{:S(2)}) collective-permute-start(bf16[1,197,1024]{2,1,0:T(8,128)(2,1)S(1)} %get-tuple-element.65), channel_id=1, source_target_pairs={{0,64},{1,65},{2,66},{3,67},{4,68},{5,69},{6,70},{7,71},{8,72},{9,... | collective-permute-start | bytes 1210376 | tf_op jit(solution)/shard_map/ppermute | solution.py:16
  213.6 68.6 %all-reduce.26.cloned.1.call-start = ((), (), s32[]{:S(2)}) async-start(), calls=%async_computation.9 | async-start | bytes 819200 | tf_op jit(solution)/shard_map/psum | solution.py:133
  256.3 74.9 %all-reduce.28.cloned.1.call-start = ((), (), s32[]{:S(2)}) async-start(), calls=%async_computation.10 | async-start | bytes 819200 | tf_op jit(solution)/shard_map/psum | solution.py:181
  305.3 78.6 %all-reduce.30.cloned.1.call-start = ((), (), s32[]{:S(2)}) async-start(), calls=%async_computation.11 | async-start | bytes 819200 | tf_op jit(solution)/shard_map/psum | solution.py:133
  331.2 19.7 %copy-start.31 = (bf16[1,1,1,197,1024]{4,1,3,2,0:T(2,128)(2,1)S(1)}, bf16[1,1,1,197,1024]{4,1,3,2,0:T(2,128)(2,1)}, u32[]{:S(2)}) copy-start(bf16[1,1,1,197,1024]{4,1,3,2,0:T(2,128)(2,1)} %get-tuple-element.76) | copy-start | bytes 1210372
  331.2 19.7 %copy-start.132 = (f32[197,2048]{1,0:T(8,128)S(1)}, f32[197,2048]{1,0:T(8,128)}, u32[]{:S(2)}) copy-start(f32[197,2048]{1,0:T(8,128)} %get-tuple-element.69) | copy-start | bytes 4841476
  335.8 15.0 %collective-permute-start.2 = (bf16[1,197,1024]{2,1,0:T(8,128)(2,1)S(1)}, bf16[1,197,1024]{2,1,0:T(8,128)(2,1)S(1)}, u32[]{:S(2)}, u32[]{:S(2)}) collective-permute-start(bf16[1,197,1024]{2,1,0:T(8,128)(2,1)S(1)} %fusion.194), channel_id=1, source_target_pairs={{64,0},{65,1},{66,2},{67,3},{68,4},{69,5},{70,6},{71,7},{72,8},{73... | collective-permute-start | bytes 1210376 | tf_op jit(solution)/shard_map/ppermute | solution.py:16
  359.8 73.1 %all-reduce.32.cloned.1.call-start = ((), (), s32[]{:S(2)}) async-start(), calls=%async_computation.12 | async-start | bytes 819200 | tf_op jit(solution)/shard_map/psum | solution.py:181
  407.4 77.8 %all-reduce.34.cloned.1.call-start = ((), (), s32[]{:S(2)}) async-start(), calls=%async_computation.13 | async-start | bytes 819200 | tf_op jit(solution)/shard_map/psum | solution.py:133
  433.0 20.6 %copy-start.131 = (f32[197,2048]{1,0:T(8,128)S(1)}, f32[197,2048]{1,0:T(8,128)}, u32[]{:S(2)}) copy-start(f32[197,2048]{1,0:T(8,128)} %get-tuple-element.93) | copy-start | bytes 4841476
  435.2 18.4 %copy-start.130 = (f32[197,2048]{1,0:T(8,128)S(1)}, f32[197,2048]{1,0:T(8,128)}, u32[]{:S(2)}) copy-start(f32[197,2048]{1,0:T(8,128)} %get-tuple-element.73) | copy-start | bytes 4841476
  438.5 15.0 %collective-permute-start.3 = (bf16[1,197,1024]{2,1,0:T(8,128)(2,1)S(1)}, bf16[1,197,1024]{2,1,0:T(8,128)(2,1)S(1)}, u32[]{:S(2)}, u32[]{:S(2)}) collective-permute-start(bf16[1,197,1024]{2,1,0:T(8,128)(2,1)S(1)} %get-tuple-element.63), channel_id=1, source_target_pairs={{64,0},{65,1},{66,2},{67,3},{68,4},{69,5},{70,6},{71,7},{72,8},{73... | collective-permute-start | bytes 1210376 | tf_op jit(solution)/shard_map/ppermute | solution.py:16
  461.1 78.9 %all-reduce.36.cloned.1.call-start = ((), (), s32[]{:S(2)}) async-start(), calls=%async_computation.18 | async-start | bytes 1638400 | tf_op jit(solution)/shard_map/psum | solution.py:78
  508.0 191.1 %reduce-scatter.7.cloned.1.call-start = ((), (), s32[]{:S(2)}) async-start(), calls=%async_computation.15 | async-start | bytes 1081344 | tf_op jit(solution)/shard_map/reduce_scatter | solution.py:268
  512.5 350.9 %reduce-scatter.5.cloned.1.call-start = ((), (), s32[]{:S(2)}) async-start(), calls=%async_computation.14 | async-start | bytes 3244032 | tf_op jit(solution)/shard_map/reduce_scatter | solution.py:265
  519.3 511.9 %reduce-scatter.9.cloned.1.call-start = ((), (), s32[]{:S(2)}) async-start(), calls=%async_computation.16 | async-start | bytes 4325376 | tf_op jit(solution)/shard_map/reduce_scatter | solution.py:274
  527.7 670.4 %reduce-scatter.11.cloned.1.call-start = ((), (), s32[]{:S(2)}) async-start(), calls=%async_computation.17 | async-start | bytes 4325376 | tf_op jit(solution)/shard_map/reduce_scatter | solution.py:277
  (128 other events, 408.6 us)
Sparse Core Ops, SparseCore 0:
  25.5 26.5 all-reduce.15
  65.9 25.4 all-reduce.17
  119.4 26.3 all-reduce.19
  159.6 25.4 all-reduce.21
  213.7 26.3 all-reduce.23
  256.4 25.6 all-reduce.25
  305.4 25.6 all-reduce.27
  359.9 23.9 all-reduce.29
  407.5 25.4 all-reduce.31
  461.3 23.9 all-reduce.33
  508.1 26.2 all-reduce.35
  536.5 162.4 reduce-scatter.6
  701.5 161.7 reduce-scatter.4
  865.6 165.5 reduce-scatter.8
  1033.4 164.6 reduce-scatter.10
where the time goes:
time: 1220 us; the launch traced here: 1210 us
  waiting for transfers between devices  852 us (70%)
  matrix products  120 us (10%)
  blocking collectives  83.1 us (7%)
  local copies, waits for them, and re-layouts  68.9 us (6%)
  other arithmetic  50.2 us (4%)
  between operations  17 us (1%)
  starting transfers between devices  14.9 us (1%)
    reduce_scatter x1, waiting for transfers between devices, per_device(): lax.psum_scatter(total_expand.astype(jnp.bfloat16), 'dp', scatter_dimensi...  166 us
    reduce_scatter x1, waiting for transfers between devices, per_device(): lax.psum_scatter(total_reduce.astype(jnp.bfloat16), 'dp', scatter_dimensi...  165 us
    reduce_scatter x1, waiting for transfers between devices, per_device(): lax.psum_scatter(total_input.astype(jnp.bfloat16), 'dp', scatter_dimensio...  163 us
    unnamed x1, blocking collectives  83.1 us
    psum x3, waiting for transfers between devices, forward_block(): lax.psum(attend_terms.astype(jnp.bfloat16), 'tensor').astype(jnp.float32)  74.1 us
    psum x3, waiting for transfers between devices, backward_block(): lax.psum(norm_two_terms.astype(jnp.bfloat16), 'tensor').astype(jnp.float32)  68.7 us
    reduce_scatter x1, waiting for transfers between devices, per_device(): lax.psum_scatter(total_output.astype(jnp.bfloat16), 'dp', scatter_dimensi...  68.3 us
    psum x2, waiting for transfers between devices, backward_block(): lax.psum(norm_one_terms.astype(jnp.bfloat16), 'tensor').astype(jnp.float32)  51.3 us
  transfers between devices with their start and end apart: 19, of which 18 were waited for; matrix products, arithmetic and copies ran while one was open for 4% of the time, Pallas kernels for 0%

commit v1 on v0

v1 whole, which is shorter than its diff:
```python
import functools

import jax
import jax.numpy as jnp
from jax import lax
from jax.experimental import pallas as pl
from jax.experimental.pallas import tpu as pltpu
from jax.sharding import PartitionSpec as P

f32 = jnp.float32
bf16 = jnp.bfloat16
MESH = pl.DeviceIdType.MESH

TOKENS = 197
PAD = 208
IMGS = 2
ROWS = IMGS * PAD
D = 1024
WIDE = 2048
HALF = 512
QKV = 3 * HALF
ROW_CHUNK = 32
N_CHUNK = ROWS // ROW_CHUNK
EPS = 1e-06

GRADS = ((64, D), (32, WIDE), (16, D), (32, QKV), (16, 256))


def _streams():
    groups = []

    def pair(m, r0, r, c0, c):
        groups.append(((m, r0, r, c0, c // 2, 0), (m, r0, r, c0 + c // 2, c // 2, 1)))

    pair(0, 0, 32, 0, 1024)
    pair(0, 32, 32, 0, 1024)
    pair(1, 0, 32, 0, 1024)
    pair(1, 0, 32, 1024, 1024)
    pair(2, 0, 16, 0, 1024)
    pair(3, 0, 32, 1024, 512)
    pair(3, 0, 32, 0, 512)
    pair(3, 0, 32, 512, 512)
    groups.append(((4, 0, 16, 0, 256, 0),))
    return groups


GROUPS = _streams()
STREAMS = [s for g in GROUPS for s in g]
BUF_NAMES = ("b1", "b2", "b3", "c1", "c2")


def _buffers(spec):
    r, h = spec[2], spec[4] // 2
    return (
        (2, 4, 2, r, h),
        (2, 2, 4, 2, r, h),
        (2, 4, r, h),
        (2, r, h),
        (2, 2, r, h),
    )


def _loop(n, body):
    def step(i, c):
        body(i)
        return c

    lax.fori_loop(0, n, step, 0)


def _add_into(dst, srcs):
    if len(dst.shape) == 2:
        v = srcs[0][...].astype(f32)
        for s in srcs[1:]:
            v = v + s[...].astype(f32)
        dst[...] = v.astype(dst.dtype)
        return

    def body(i):
        v = srcs[0][i].astype(f32)
        for s in srcs[1:]:
            v = v + s[i].astype(f32)
        dst[i] = v.astype(dst.dtype)

    _loop(dst.shape[0], body)


class _Stream:
    def __init__(self, index, spec, grads, bufs, outs, sems, coords):
        self.index, self.spec, self.grads, self.b, self.outs = index, spec, grads, bufs, outs
        self.send_sem, self.recv_sem = sems
        self.H = self.b["b2"].at[0]
        self.K = self.b["b3"]
        self.co = coords

    def g(self, j, half):
        m, r0, r, c0, c, order = self.spec
        h = c // 2
        grad = self.grads[m]
        rows, cols = pl.ds(r0, r), pl.ds(c0 + half * h, h)
        return grad.at[j, :, :, rows, cols] if order == 0 else grad.at[:, j, :, rows, cols]

    def kk(self, j, half):
        return self.K.at[half, j]

    def peer(self, axis, d):
        z, x, y = self.co
        if axis == "y":
            y = 1 - y
        elif axis == "z":
            z = lax.rem(z + d + 4, 4)
        else:
            x = lax.rem(x + d + 4, 4)
        return {"dp": z * 8 + x * 2 + y}

    def copy(self, k, src, dst, axis, d):
        return pltpu.make_async_remote_copy(
            src_ref=src,
            dst_ref=dst,
            send_sem=self.send_sem.at[self.index, k],
            recv_sem=self.recv_sem.at[self.index, k],
            device_id=self.peer(axis, d),
            device_id_type=MESH,
        )

    def ring(self, phase):
        axis = ("zx", "xz")[self.spec[5]][phase]
        p = self.co[0] if axis == "z" else self.co[1]
        src = (self.g, self.kk)[phase]
        one, two = (self.b["b1"], self.b["b2"]) if phase == 0 else (self.b["c1"], self.b["c2"])
        return axis, (lambda d: lax.rem(p + d + 4, 4)), src, one, two, 7 * phase

    def ring_copy(self, phase, n):
        axis, at, src, one, two, k = self.ring(phase)
        source, dst, step = (
            (lambda: src(at(2), 0), one.at[0], 1),
            (lambda: src(at(2), 1), one.at[1], -1),
            (lambda: src(at(1), 1), two.at[0, 1], 1),
            (lambda: src(at(-1), 0), two.at[1, 0], -1),
            (lambda: one.at[0], two.at[0, 0], 1),
            (lambda: one.at[1], two.at[1, 1], -1),
        )[n]
        return self.copy(k + n, source(), dst, axis, step)

    def ring_start(self, phase):
        for n in range(4):
            self.ring_copy(phase, n).start()

    def ring_mid(self, phase):
        axis, at, src, one, two, k = self.ring(phase)
        self.ring_copy(phase, 0).wait_recv()
        _add_into(one.at[0], [one.at[0], src(at(1), 0)])
        self.ring_copy(phase, 4).start()
        self.ring_copy(phase, 1).wait_recv()
        _add_into(one.at[1], [one.at[1], src(at(-1), 1)])
        self.ring_copy(phase, 5).start()

    def ring_end(self, phase):
        for n in range(2, 6):
            self.ring_copy(phase, n).wait_recv()

    def y_copy(self):
        return self.copy(6, self.H.at[:, :, 1 - self.co[2]], self.b["b3"], "y", 0)

    def stage(self, n):
        getattr(self, "stage%d" % n)()

    def stage0(self):
        self.ring_start(0)

    def stage1(self):
        self.ring_mid(0)

    def stage2(self):
        self.ring_end(0)
        p = self.ring(0)[1](0)
        two = self.b["b2"]
        for half in (0, 1):
            _add_into(self.H.at[half], [self.g(p, half), two.at[0, half], two.at[1, half]])
        self.y_copy().start()

    def stage3(self):
        self.y_copy().wait_recv()
        for half in (0, 1):
            _add_into(
                self.K.at[half],
                [self.H.at[half, :, self.co[2]], self.b["b3"].at[half]],
            )
        self.ring_start(1)

    def stage4(self):
        self.ring_mid(1)

    def stage5(self):
        self.ring_end(1)
        p = self.ring(1)[1](0)
        two = self.b["c2"]
        m, r0, r, c0, c, order = self.spec
        h = c // 2
        for half in (0, 1):
            v = self.K[half, p].astype(f32) + two[0, half].astype(f32)
            self.outs[m][pl.ds(r0, r), pl.ds(c0 + half * h, h)] = v + two[1, half].astype(f32)

    def drain(self):
        for phase in (0, 1):
            for n in range(6):
                self.ring_copy(phase, n).wait_send()
        self.y_copy().wait_send()


def _nn(a, b):
    return lax.dot_general(a, b, (((1,), (0,)), ((), ())), preferred_element_type=f32)


def _nt(a, b):
    return lax.dot_general(a, b, (((1,), (1,)), ((), ())), preferred_element_type=f32)


def _tn(a, b):
    return lax.dot_general(a, b, (((0,), (0,)), ((), ())), preferred_element_type=f32)


def _norm(v):
    centre = v - jnp.mean(v, axis=-1, keepdims=True)
    inv = lax.rsqrt(jnp.mean(centre * centre, axis=-1, keepdims=True) + EPS)
    return centre * inv, inv


def _norm_back(upstream, hat, inv, gain):
    q = upstream * gain
    return inv * (
        q - jnp.mean(q, axis=-1, keepdims=True) - hat * jnp.mean(q * hat, axis=-1, keepdims=True)
    )


def _cols(i, n):
    return pl.ds(pl.multiple_of(i * n, n), n)


def _kernel(*refs):
    (images, cotangent, gain_one, gain_two, wqkv_in, wo_in, w1_in, w2_in) = refs[:8]
    (y_ref, ig_ref, o_w2, o_w1, o_wo, o_qkv, o_gain) = refs[8:15]
    rest = refs[15:]
    (
        wqkv, wo, w1, w2, g_w2, g_w1, g_wo, g_qkv, g_gain,
        xb, eb, hin, n1, pr, pb, mx, mid, n2, act, gp, eg, mlow, pg, sendb, recvb, gacc,
        load_sem, x_ss, x_rs, hop_sem, rs_ss, rs_rs,
    ) = rest[:32]
    ring_bufs = rest[32:]

    section = lax.axis_index("section")
    tensor = lax.axis_index("tensor")
    dp = lax.axis_index("dp")
    z, x, y = dp // 8, lax.rem(dp // 2, 4), lax.rem(dp, 2)

    loads = [
        pltpu.make_async_copy(src, dst, load_sem.at[i])
        for i, (src, dst) in enumerate(
            ((images, xb), (wqkv_in, wqkv), (wo_in, wo), (w1_in, w1), (w2_in, w2), (cotangent, eb))
        )
    ]
    for c in loads:
        c.start()

    barrier = pltpu.get_barrier_semaphore()

    def r4(v):
        return lax.rem(v + 4, 4)

    for peer in (
        {"tensor": 1 - tensor},
        {"section": 1 - section},
        {"dp": r4(z + 1) * 8 + x * 2 + y},
        {"dp": r4(z - 1) * 8 + x * 2 + y},
        {"dp": z * 8 + r4(x + 1) * 2 + y},
        {"dp": z * 8 + r4(x - 1) * 2 + y},
        {"dp": z * 8 + x * 2 + 1 - y},
    ):
        pl.semaphore_signal(barrier, inc=1, device_id=peer, device_id_type=MESH)
    pl.semaphore_wait(barrier, 7)

    def exchange(par, chunk):
        part = (slice(None), pl.ds(chunk * 512, 512))
        return pltpu.make_async_remote_copy(
            src_ref=sendb.at[par].at[part],
            dst_ref=recvb.at[par].at[part],
            send_sem=x_ss.at[par, chunk],
            recv_sem=x_rs.at[par, chunk],
            device_id={"tensor": 1 - tensor},
            device_id_type=MESH,
        )

    def exchange_wait(par):
        for chunk in (0, 1):
            exchange(par, chunk).wait()

    own_half = pl.ds(pl.multiple_of(tensor * 512, 512), 512)
    other_half = pl.ds(pl.multiple_of((1 - tensor) * 512, 512), 512)

    def hop(src):
        return pltpu.make_async_remote_copy(
            src_ref=src.at[:, own_half],
            dst_ref=hin.at[:, own_half],
            send_sem=hop_sem.at[0],
            recv_sem=hop_sem.at[1],
            device_id={"section": 1 - section},
            device_id_type=MESH,
        )

    def forward_half(cols):
        return pltpu.make_async_remote_copy(
            src_ref=hin.at[:, cols],
            dst_ref=hin.at[:, cols],
            send_sem=hop_sem.at[2],
            recv_sem=hop_sem.at[3],
            device_id={"tensor": 1 - tensor},
            device_id_type=MESH,
        )

    def receive(src, dst):
        hop(src).wait_recv()
        forward_half(own_half).start()
        forward_half(own_half).wait_send()
        forward_half(other_half).wait_recv()

        def body(i):
            rows = _cols(i, ROW_CHUNK)
            dst[rows, :] = hin[rows, :]

        _loop(N_CHUNK, body)

    lane = lax.broadcasted_iota(jnp.int32, (1, 128), 1)
    head_masks = ((lane < 64).astype(bf16), (lane >= 64).astype(bf16))
    key_ok = lax.broadcasted_iota(jnp.int32, (PAD, PAD), 1) < TOKENS

    def forward(tick):
        @pl.when(jnp.logical_and(tick == 1, section == 1))
        def _():
            receive(y_ref, xb)

        def ln_one(i):
            rows = _cols(i, ROW_CHUNK)
            hat, inv = _norm(xb[rows, :].astype(f32))
            n1[rows, :] = (hat * gain_one[...]).astype(bf16)

        _loop(N_CHUNK, ln_one)

        @pl.when(tick == 0)
        def _():
            loads[1].wait()

        def project(i):
            pr[:, _cols(i, 512)] = _nn(n1[...], wqkv[:, _cols(i, 512)]).astype(bf16)

        _loop(3, project)

        def attend(i):
            img, pair_i = i // 4, lax.rem(i, 4)
            rows = _cols(img, PAD)
            q = pr[rows, _cols(pair_i, 128)]
            k = pr[rows, _cols(pair_i + 4, 128)]
            v = pr[rows, _cols(pair_i + 8, 128)]
            total = None
            for h in (0, 1):
                s = _nt(q * head_masks[h], k) * 0.125
                s = jnp.where(key_ok, s, -1e30)
                e = jnp.exp(s - jnp.max(s, axis=-1, keepdims=True))
                p = (e / jnp.sum(e, axis=-1, keepdims=True)).astype(bf16)
                pb[i * 2 + h] = p
                t = _nn(p, v * head_masks[h])
                total = t if total is None else total + t
            mx[rows, _cols(pair_i, 128)] = total.astype(bf16)

        _loop(8, attend)

        @pl.when(tick == 0)
        def _():
            loads[2].wait()

        for chunk in (0, 1):
            part = pl.ds(chunk * 512, 512)
            sendb[0, :, part] = _nn(mx[...], wo[:, part]).astype(bf16)
            exchange(0, chunk).start()
        exchange_wait(0)

        def ln_two(i):
            rows = _cols(i, ROW_CHUNK)
            m = xb[rows, :].astype(f32) + (
                sendb[0, rows, :].astype(f32) + recvb[0, rows, :].astype(f32)
            )
            mid[rows, :] = m
            hat, inv = _norm(m)
            n2[rows, :] = (hat * gain_two[...]).astype(bf16)

        _loop(N_CHUNK, ln_two)

        @pl.when(tick == 0)
        def _():
            loads[3].wait()

        def expand(i):
            part = _cols(i, 256)
            e = _nn(n2[...], w1[:, part])
            phi = 0.5 * (1.0 + lax.erf(e * 0.7071067811865476))
            act[:, part] = (e * phi).astype(bf16)
            gp[:, part] = (phi + e * (jnp.exp(-0.5 * e * e) * 0.3989422804014327)).astype(bf16)

        _loop(8, expand)

        @pl.when(tick == 0)
        def _():
            loads[4].wait()

        for chunk in (0, 1):
            part = pl.ds(chunk * 512, 512)
            sendb[1, :, part] = _nn(act[...], w2[:, part]).astype(bf16)
            exchange(1, chunk).start()
        exchange_wait(1)

        def finish(i):
            rows = _cols(i, ROW_CHUNK)
            v = mid[rows, :] + (sendb[1, rows, :].astype(f32) + recvb[1, rows, :].astype(f32))
            y_ref[rows, :] = v.astype(bf16)

        _loop(N_CHUNK, finish)

        @pl.when(jnp.logical_and(tick == 0, section == 0))
        def _():
            hop(y_ref).start()
            hop(y_ref).wait_send()

    loads[0].wait()
    _loop(2, forward)
    loads[5].wait()

    grads = (g_w2, g_w1, g_wo, g_qkv, g_gain)
    outs = (o_w2, o_w1, o_wo, o_qkv, o_gain)
    nb = len(BUF_NAMES)
    streams = [
        _Stream(
            i, spec, grads, dict(zip(BUF_NAMES, ring_bufs[i * nb : (i + 1) * nb])), outs,
            (rs_ss, rs_rs), (z, x, y),
        )
        for i, spec in enumerate(STREAMS)
    ]
    groups, count = [], 0
    for g in GROUPS:
        groups.append(streams[count : count + len(g)])
        count += len(g)

    def start_group(i):
        for s in groups[i]:
            s.stage(0)

    def pump(tick):
        for st in (1, 2, 3, 4, 5):
            i = tick - st
            if 0 <= i < len(groups):
                for s in groups[i]:
                    s.stage(st)

    def pack_gain(row, half):
        lanes = lax.broadcasted_iota(jnp.int32, (1024, 128), 0)
        pick = (lax.rem(lanes, 32) == lax.broadcasted_iota(jnp.int32, (1024, 128), 1)).astype(bf16)
        for zz in range(4):
            r = lax.broadcasted_iota(jnp.int32, (128, 1024), 0) // 16 + zz * 8
            c = lax.broadcasted_iota(jnp.int32, (128, 1024), 1) // 32
            spread = jnp.where(r == c, row, 0.0).astype(bf16)
            g_gain[zz, :, :, :, pl.ds(half * 128, 128)] = (
                _nn(spread, pick).astype(bf16).reshape(4, 2, 16, 128)
            )

    def backward(tick):
        last = tick == 1

        @pl.when(jnp.logical_and(last, section == 0))
        def _():
            receive(ig_ref, eb)

        @pl.when(last)
        def _():
            def tile(i):
                for n in (0, 1):
                    part = pl.ds(n * 512, 512)
                    t = _tn(act[:, _cols(i, 256)], eb[:, part]).astype(bf16)
                    g_w2[i // 2, pl.ds(lax.rem(i, 2) * 2, 2), :, :, part] = t.reshape(2, 2, 64, 512)

            _loop(8, tile)
            start_group(0)
            start_group(1)

        def expand_back(i):
            part = _cols(i, 256)
            d = _nt(eb[...], w2[part, :])
            eg[:, part] = (d * gp[:, part].astype(f32)).astype(bf16)

        _loop(8, expand_back)

        @pl.when(last)
        def _():
            pump(1)

        for chunk in (0, 1):
            part = pl.ds(chunk * 512, 512)
            sendb[0, :, part] = _nt(eg[...], w1[part, :]).astype(bf16)
            exchange(0, chunk).start()

        @pl.when(last)
        def _():
            def tile(i):
                for n in range(4):
                    part = pl.ds(n * 512, 512)
                    t = _tn(n2[:, _cols(i, 256)], eg[:, part]).astype(bf16)
                    g_w1[i, :, :, :, part] = t.reshape(4, 2, 32, 512)

            _loop(4, tile)
            start_group(2)
            start_group(3)

        exchange_wait(0)
        gacc[...] = jnp.zeros_like(gacc)

        def ln_two_back(i):
            rows = _cols(i, ROW_CHUNK)
            dn = sendb[0, rows, :].astype(f32) + recvb[0, rows, :].astype(f32)
            hat, inv = _norm(mid[rows, :])
            gacc[0:1, :] += jnp.sum(dn * hat, axis=0, keepdims=True)
            m = eb[rows, :].astype(f32) + _norm_back(dn, hat, inv, gain_two[...])
            mlow[rows, :] = m.astype(bf16)

        _loop(N_CHUNK, ln_two_back)

        sendb[1, :, pl.ds(0, HALF)] = _nt(mlow[...], wo[...]).astype(bf16)

        @pl.when(last)
        def _():
            pump(2)

            def tile(i):
                for n in (0, 1):
                    part = pl.ds(n * 512, 512)
                    t = _tn(mx[:, _cols(i, 256)], mlow[:, part]).astype(bf16)
                    g_wo[pl.ds(i * 2, 2), :, :, :, part] = t.reshape(2, 4, 2, 16, 512)

            _loop(2, tile)
            start_group(4)
            pump(3)

        def attend_back(i):
            img, pair_i = i // 4, lax.rem(i, 4)
            rows = _cols(img, PAD)
            q = pr[rows, _cols(pair_i, 128)]
            k = pr[rows, _cols(pair_i + 4, 128)]
            v = pr[rows, _cols(pair_i + 8, 128)]
            do = sendb[1, rows, _cols(pair_i, 128)]
            sums = [None, None, None]
            for h in (0, 1):
                mask = head_masks[h]
                p = pb[i * 2 + h]
                pf = p.astype(f32)
                doh = do * mask
                dpr = _nt(doh, v)
                inner = jnp.sum(dpr * pf, axis=-1, keepdims=True)
                ds = (pf * (dpr - inner)).astype(bf16)
                for j, t in enumerate((_nn(ds, k * mask), _tn(ds, q * mask), _tn(p, doh))):
                    sums[j] = t if sums[j] is None else sums[j] + t
            for j, scale in enumerate((0.125, 0.125, 1.0)):
                pg[rows, _cols(pair_i + 4 * j, 128)] = (sums[j] * scale).astype(bf16)

        _loop(8, attend_back)

        @pl.when(last)
        def _():
            pump(4)

        for chunk in (0, 1):
            part = pl.ds(chunk * 512, 512)
            sendb[1, :, part] = _nt(pg[...], wqkv[part, :]).astype(bf16)
            exchange(1, chunk).start()

        @pl.when(last)
        def _():
            def tile(i):
                for n in range(3):
                    part = pl.ds(n * 512, 512)
                    t = _tn(n1[:, _cols(i, 256)], pg[:, part]).astype(bf16)
                    g_qkv[i, :, :, :, part] = t.reshape(4, 2, 32, 512)

            _loop(4, tile)
            for i in (5, 6, 7):
                start_group(i)

        exchange_wait(1)

        def ln_one_back(i):
            rows = _cols(i, ROW_CHUNK)
            dn = sendb[1, rows, :].astype(f32) + recvb[1, rows, :].astype(f32)
            hat, inv = _norm(xb[rows, :].astype(f32))
            gacc[1:2, :] += jnp.sum(dn * hat, axis=0, keepdims=True)
            m = mlow[rows, :].astype(f32) + _norm_back(dn, hat, inv, gain_one[...])
            ig_ref[rows, :] = m.astype(bf16)

        _loop(N_CHUNK, ln_one_back)

        @pl.when(jnp.logical_and(tick == 0, section == 1))
        def _():
            hop(ig_ref).start()
            hop(ig_ref).wait_send()

    _loop(2, backward)
    pack_gain(gacc[1:2, :], 0)
    pack_gain(gacc[0:1, :], 1)
    start_group(8)
    for tick in range(5, len(groups) + 5):
        pump(tick)
    for s in streams:
        s.drain()


def _call(*args):
    vmem = pl.BlockSpec(memory_space=pltpu.VMEM)
    hbm = pl.BlockSpec(memory_space=pl.ANY)
    out_shape = [jax.ShapeDtypeStruct((ROWS, D), bf16)] * 2 + [
        jax.ShapeDtypeStruct(s, f32) for s in GRADS
    ]
    scratch = [
        pltpu.VMEM((D, QKV), bf16),
        pltpu.VMEM((HALF, D), bf16),
        pltpu.VMEM((D, WIDE), bf16),
        pltpu.VMEM((WIDE, D), bf16),
    ]
    scratch += [pltpu.VMEM((4, 4, 2) + s, bf16) for s in GRADS]
    scratch += [
        pltpu.VMEM((ROWS, D), bf16),
        pltpu.VMEM((ROWS, D), bf16),
        pltpu.VMEM((ROWS, D), bf16),
        pltpu.VMEM((ROWS, D), bf16),
        pltpu.VMEM((ROWS, QKV), bf16),
        pltpu.VMEM((16, PAD, PAD), bf16),
        pltpu.VMEM((ROWS, HALF), bf16),
        pltpu.VMEM((ROWS, D), f32),
        pltpu.VMEM((ROWS, D), bf16),
        pltpu.VMEM((ROWS, WIDE), bf16),
        pltpu.VMEM((ROWS, WIDE), bf16),
        pltpu.VMEM((ROWS, WIDE), bf16),
        pltpu.VMEM((ROWS, D), bf16),
        pltpu.VMEM((ROWS, QKV), bf16),
        pltpu.VMEM((2, ROWS, D), bf16),
        pltpu.VMEM((2, ROWS, D), bf16),
        pltpu.VMEM((8, D), f32),
        pltpu.SemaphoreType.DMA((6,)),
        pltpu.SemaphoreType.DMA((2, 2)),
        pltpu.SemaphoreType.DMA((2, 2)),
        pltpu.SemaphoreType.DMA((4,)),
        pltpu.SemaphoreType.DMA((len(STREAMS), 13)),
        pltpu.SemaphoreType.DMA((len(STREAMS), 13)),
    ]
    for s in STREAMS:
        scratch += [pltpu.VMEM(b, bf16) for b in _buffers(s)]
    return pl.pallas_call(
        _kernel,
        out_shape=out_shape,
        in_specs=[hbm, hbm, vmem, vmem, hbm, hbm, hbm, hbm],
        out_specs=[vmem] * len(out_shape),
        scratch_shapes=scratch,
        compiler_params=pltpu.CompilerParams(
            collective_id=0, has_side_effects=True, vmem_limit_bytes=63 << 20
        ),
    )(*args)


def per_device(
    images, cotangent, shard_count, slot_order, attend_gain, attend_input, attend_output,
    feed_gain, feed_expand, feed_reduce,
):
    slots = jnp.arange(IMGS, dtype=jnp.int32)
    matches = slot_order[0][:, None] == slots[None, :]
    taken = (slots < shard_count[0])[:, None]
    live = jnp.any(matches & taken, axis=0).astype(bf16)

    def padded(v):
        return jnp.pad(v, ((0, 0), (0, PAD - TOKENS), (0, 0))).reshape(ROWS, D)

    top = cotangent[0, :, 0] * live[:, None, None]
    y, ig, d_w2, d_w1, d_wo, d_qkv, d_gain = _call(
        padded(images[0, :, 0]), padded(top), attend_gain, feed_gain,
        attend_input[0].reshape(D, QKV), attend_output[0], feed_expand[0], feed_reduce[0],
    )

    def cut(v):
        return v.reshape(IMGS, PAD, D)[:, :TOKENS].reshape(1, 1, IMGS, 1, TOKENS, D)

    return (
        cut(y), cut(ig), d_gain[0:1, 0:32], d_qkv.reshape(1, 32, 3, HALF), d_wo[None],
        d_gain[0:1, 128:160], d_w1[None], d_w2[None],
    )


def solution(mesh):
    in_specs = (
        P("dp", None, None, None, None),
        P("dp", None, None, None, None),
        P("dp"),
        P("dp", None),
        P("section", None),
        P("section", None, None, "tensor"),
        P("section", "tensor", None),
        P("section", None),
        P("section", None, "tensor"),
        P("section", "tensor", None),
    )
    out_specs = (
        P("section", "dp", None, None, None, None),
        P("section", "dp", None, None, None, None),
        P("section", "dp"),
        P("section", "dp", None, "tensor"),
        P("section", ("tensor", "dp"), None),
        P("section", "dp"),
        P("section", "dp", "tensor"),
        P("section", ("tensor", "dp"), None),
    )
    return jax.shard_map(
        per_device, mesh=mesh, in_specs=in_specs, out_specs=out_specs, check_vma=False
    )
```

time: 1220 us -> 215 us (0.18); the launches traced: 1210 us -> 214 us
  waiting for transfers between devices: 852 us -> 0 us
  Pallas kernels: 0 us -> 193 us
  matrix products: 120 us -> 0 us
  blocking collectives: 83.1 us -> 0 us
  local copies, waits for them, and re-layouts: 68.9 us -> 18 us
  other arithmetic: 50.2 us -> 2 us
  between operations: 17 us -> 1.47 us
  starting transfers between devices: 14.9 us -> 0 us
    reduce_scatter x4 -> x0, waiting for transfers between devices: 563 us -> none  [the longest x1 166 us: per_device(): lax.psum_scatter(total_expand.astype(jnp.bfloat16), 'dp', scatter_dimensi...]
    psum x11 -> x0, waiting for transfers between devices: 245 us -> none  [the longest x3 74.1 us: forward_block(): lax.psum(attend_terms.astype(jnp.bfloat16), 'tensor').astype(jnp.float32)]
    pallas_call x0 -> x1, Pallas kernels: none -> 193 us  [_call(): pl.pallas_call(_kernel, out_shape=out_shape, in_specs=[hbm, hbm, vmem, vm...]
    dot_general x54 -> x0, matrix products: 120 us -> none  [the longest x3 24.5 us: forward_block(): jnp.einsum('cld,df->clf', norm_two, feed_expand, preferred_element_type=j...]
    unnamed x1 -> x0, blocking collectives: 83.1 us -> none
    ppermute x4 -> x0, waiting for transfers between devices: 44.1 us -> none  [shifted(): lax.ppermute(value, axis, [(source, source + steps) for source in range(f...]
    slice x15 -> x3, local copies, waits for them, and re-layouts: 27.8 us -> 3.7 us  [the longest x2 2.5 us: cut(): return v.reshape(IMGS, PAD, D)[:, :TOKENS].reshape(1, 1, IMGS, 1, TOKENS, D)]
    reduce_sum x22 -> x0, other arithmetic: 23.6 us -> none  [the longest x3 7.1 us: backward_block(): feed_gain_part = jnp.sum(norm_two_gradient * hat_two, axis=(0, 1))]
  transfers between devices with their start and end apart: 19 -> 0, of which waited for: 18 -> 0; matrix products, arithmetic and copies ran while one was open for 4% -> 0% of each run, Pallas kernels for 0% -> 0%
where the time goes in v1:
time: 215 us; the launch traced here: 214 us
  Pallas kernels  193 us (90%)
  local copies, waits for them, and re-layouts  18 us (8%)
    pallas_call x1, Pallas kernels, _call(): pl.pallas_call(_kernel, out_shape=out_shape, in_specs=[hbm, hbm, vmem, vm...  193 us
    unnamed x19, local copies, waits for them, and re-layouts  6.4 us

profile of v1, /device:TPU:0, one launch (start us, length us, event | category | flops | bytes accessed | tf_op | source)
XLA Modules:
  0.0 214.5 jit_solution(6974071321124874218)
XLA Ops:
  0.6 3.2 %copy.33 = bf16[1,1024,3,512]{1,3,2,0:T(8,128)(2,1)S(1)} copy(bf16[1,1024,3,512]{3,1,2,0:T(8,128)(2,1)} %param.15) | data formatting | bytes 6291456 | tf_op args[5]
  3.8 0.0 copy-start.5
  3.8 3.0 %copy.34.refs_4_ = bf16[1024,1536]{1,0:T(8,128)(2,1)} copy(bf16[1024,1536]{0,1:T(8,128)(2,1)S(1)} %bitcast.21) | data formatting | bytes 6291456 | tf_op jit(solution)/shard_map/reshape;squeeze | solution.py:687
  7.5 0.0 copy-done.5
  7.5 0.1 and_reduce_fusion
  7.6 1.9 bitcast_multiply_fusion
  9.5 0.2 copy.41
  9.8 1.0 pad.8.clone
  10.7 0.0 copy-done
  10.7 0.2 copy.40
  10.9 1.0 pad.7.clone
  11.9 193.0 %shard_map.161 = (bf16[416,1024]{1,0:T(8,128)(2,1)}, bf16[416,1024]{1,0:T(8,128)(2,1)}, f32[64,1024]{1,0:T(8,128)}, f32[32,2048]{1,0:T(8,128)}, f32[16,1024]{1,0...) custom-call(bf16[416,1024]{1,0:T(8,128)(2,1)} %bitcast.25, bf16[416,1024]{1,0:T(8,128)(2,1)} %bitcast.24, ...), custom_call_target="tpu_custom_call" | custom-call | tf_op jit(solution)/shard_map/pallas_call | solution.py:660
  205.0 0.0 copy-start.3
  205.0 1.2 slice.16
  206.2 0.0 copy-start.4
  206.3 1.3 slice.17
  207.5 2.8 %copy_bitcast_fusion = (bf16[1,1,2,1,197,1024]{5,2,4,3,1,0:T(2,128)(2,1)}, bf16[1,1,2,1,197,1024]{5,2,4,3,1,0:T(2,128)(2,1)}) fusion(bf16[2,197,1024]{2,1,0:T(8,128)(2,1)S(1)} %slice.17, bf16[2,197,1024]{2,1,0:T(8,128)(2,1)S(1)} %slice.16), kind=kLoop, calls=%fused_computation | loop fusion | bytes 3227648 | tf_op jit(solution)/shard_map/reshape | solution.py:691
  210.3 1.2 fusion
  211.5 0.0 copy-done.3
  211.5 0.1 reshape.51
  211.7 0.7 copy.37
  212.4 0.6 copy.48
  213.1 0.7 copy.49
  213.8 0.7 copy.50
  (8 shorter events, 0.0 us)
Async XLA Ops:
  3.8 3.7 %copy-start.5 = (s32[1,2]{1,0:T(1,128)S(1)}, s32[1,2]{1,0:T(1,128)}, u32[]{:S(2)}) copy-start(s32[1,2]{1,0:T(1,128)} %param.13) | copy-start | bytes 28
  6.8 3.9 %copy-start = (bf16[1,2,1,197,1024]{4,1,3,2,0:T(2,128)(2,1)S(1)}, bf16[1,2,1,197,1024]{4,1,3,2,0:T(2,128)(2,1)}, u32[]{:S(2)}) copy-start(bf16[1,2,1,197,1024]{4,1,3,2,0:T(2,128)(2,1)} %param.10) | copy-start | bytes 2420740
  205.0 6.6 %copy-start.3 = (f32[32,1536]{1,0:T(8,128)S(1)}, f32[32,1536]{1,0:T(8,128)}, u32[]{:S(2)}) copy-start(f32[32,1536]{1,0:T(8,128)} %get-tuple-element.18) | copy-start | bytes 589828
  206.2 6.2 %copy-start.4 = (f32[16,1024]{1,0:T(8,128)S(1)}, f32[16,1024]{1,0:T(8,128)}, u32[]{:S(2)}) copy-start(f32[16,1024]{1,0:T(8,128)} %get-tuple-element.19) | copy-start | bytes 196612
  206.2 6.8 %copy-start.2 = (f32[32,2048]{1,0:T(8,128)S(1)}, f32[32,2048]{1,0:T(8,128)}, u32[]{:S(2)}) copy-start(f32[32,2048]{1,0:T(8,128)} %get-tuple-element.20) | copy-start | bytes 786436
  206.3 7.5 %copy-start.1 = (f32[64,1024]{1,0:T(8,128)S(1)}, f32[64,1024]{1,0:T(8,128)}, u32[]{:S(2)}) copy-start(f32[64,1024]{1,0:T(8,128)} %get-tuple-element.21) | copy-start | bytes 786436

commit v2 on v1

v2 whole, which is shorter than its diff:
```python
import functools

import jax
import jax.numpy as jnp
from jax import lax
from jax.experimental import pallas as pl
from jax.experimental.pallas import tpu as pltpu
from jax.sharding import PartitionSpec as P

f32 = jnp.float32
bf16 = jnp.bfloat16
MESH = pl.DeviceIdType.MESH

TOKENS = 197
PAD = 208
IMGS = 2
ROWS = IMGS * PAD
D = 1024
WIDE = 2048
HALF = 512
QKV = 3 * HALF
ROW_CHUNK = 32
N_CHUNK = ROWS // ROW_CHUNK
EPS = 1e-06

GRADS = ((64, D), (32, WIDE), (16, D), (32, QKV), (16, 256))


def _streams():
    groups = []

    def pair(m, r0, r, c0, c, order=0):
        groups.append(((m, r0, r, c0, c // 2, order), (m, r0, r, c0 + c // 2, c // 2, order + 1)))

    pair(0, 0, 32, 0, 1024)
    pair(0, 32, 32, 0, 1024, 2)
    pair(1, 0, 32, 0, 1024)
    pair(1, 0, 32, 1024, 1024)
    pair(2, 0, 16, 0, 1024)
    pair(3, 0, 32, 1024, 512)
    pair(3, 0, 32, 0, 512)
    pair(3, 0, 32, 512, 512)
    groups.append(((4, 0, 16, 0, 256, 0),))
    return groups


GROUPS = _streams()
STEPS = {
    "eb0": (),
    "W2": ((0, 0), (1, 0)),
    "eb1": (),
    "et": ((0, 1),),
    "W1": ((2, 0), (3, 0)),
    "ln2": ((0, 2),),
    "Wo": ((4, 0),),
    "at0": ((2, 1),),
    "at1": (),
    "it": ((3, 1),),
    "QKV": ((4, 1), (5, 0)),
    "ln1": ((1, 1),),
    "gain": (),
    "tail": ((6, 0), (2, 2), (7, 0), (0, 3), (3, 2), (4, 2), (5, 1), (8, 0), (2, 3), (1, 2), (6, 1), (3, 3), (7, 1), (0, 4), (4, 3), (5, 2), (8, 1), (2, 4), (1, 3), (6, 2), (3, 4), (5, 3), (7, 2), (0, 5), (4, 4), (8, 2), (2, 5), (1, 4), (3, 5), (5, 4), (6, 3), (4, 5), (1, 5), (5, 5), (6, 4), (7, 3), (8, 3), (6, 5), (7, 4), (8, 4), (7, 5), (8, 5)),
}
STREAMS = [s for g in GROUPS for s in g]
BUF_NAMES = ("b1", "b2", "b3", "c1", "c2")


def _buffers(spec):
    r, h = spec[2], spec[4] // 2
    if spec[5] >= 2:
        return ((2, 4, r, h), (2, 2, 4, r, h), (4, 4, r, 2 * h), (2, r, h), (2, 2, r, h))
    return (
        (2, 4, 2, r, h),
        (2, 2, 4, 2, r, h),
        (2, 4, r, h),
        (2, r, h),
        (2, 2, r, h),
    )


def _loop(n, body):
    def step(i, c):
        body(i)
        return c

    lax.fori_loop(0, n, step, 0)


def _add_into(dst, srcs):
    if len(dst.shape) == 2:
        v = srcs[0][...].astype(f32)
        for s in srcs[1:]:
            v = v + s[...].astype(f32)
        dst[...] = v.astype(dst.dtype)
        return

    def body(i):
        v = srcs[0][i].astype(f32)
        for s in srcs[1:]:
            v = v + s[i].astype(f32)
        dst[i] = v.astype(dst.dtype)

    _loop(dst.shape[0], body)


class _Stream:
    def __init__(self, index, spec, grads, bufs, outs, sems, coords):
        self.index, self.spec, self.grads, self.b, self.outs = index, spec, grads, bufs, outs
        self.send_sem, self.recv_sem = sems
        self.H = self.b["b2"].at[0]
        self.K = self.b["b3"]
        self.y_first = spec[5] >= 2
        self.co = coords

    def g(self, j, half):
        m, r0, r, c0, c, order = self.spec
        h = c // 2
        grad = self.grads[m]
        rows, cols = pl.ds(r0, r), pl.ds(c0 + half * h, h)
        if self.y_first:
            cols = pl.ds(half * h, h)
            return self.K.at[j, :, :, cols] if order == 2 else self.K.at[:, j, :, cols]
        return grad.at[j, :, :, rows, cols] if order == 0 else grad.at[:, j, :, rows, cols]

    def kk(self, j, half):
        return self.H.at[half, j] if self.y_first else self.K.at[half, j]

    def peer(self, axis, d):
        z, x, y = self.co
        if axis == "y":
            y = 1 - y
        elif axis == "z":
            z = lax.rem(z + d + 4, 4)
        else:
            x = lax.rem(x + d + 4, 4)
        return {"dp": z * 8 + x * 2 + y}

    def copy(self, k, src, dst, axis, d):
        return pltpu.make_async_remote_copy(
            src_ref=src,
            dst_ref=dst,
            send_sem=self.send_sem.at[self.index, k],
            recv_sem=self.recv_sem.at[self.index, k],
            device_id=self.peer(axis, d),
            device_id_type=MESH,
        )

    def ring(self, phase):
        axis = ("zx", "xz")[self.spec[5] % 2][phase]
        p = self.co[0] if axis == "z" else self.co[1]
        src = (self.g, self.kk)[phase]
        one, two = (self.b["b1"], self.b["b2"]) if phase == 0 else (self.b["c1"], self.b["c2"])
        return axis, (lambda d: lax.rem(p + d + 4, 4)), src, one, two, 7 * phase

    def ring_copy(self, phase, n):
        axis, at, src, one, two, k = self.ring(phase)
        source, dst, step = (
            (lambda: src(at(2), 0), one.at[0], 1),
            (lambda: src(at(2), 1), one.at[1], -1),
            (lambda: src(at(1), 1), two.at[0, 1], 1),
            (lambda: src(at(-1), 0), two.at[1, 0], -1),
            (lambda: one.at[0], two.at[0, 0], 1),
            (lambda: one.at[1], two.at[1, 1], -1),
        )[n]
        return self.copy(k + n, source(), dst, axis, step)

    def ring_start(self, phase):
        for n in range(4):
            self.ring_copy(phase, n).start()

    def ring_mid(self, phase):
        axis, at, src, one, two, k = self.ring(phase)
        self.ring_copy(phase, 0).wait_recv()
        _add_into(one.at[0], [one.at[0], src(at(1), 0)])
        self.ring_copy(phase, 4).start()
        self.ring_copy(phase, 1).wait_recv()
        _add_into(one.at[1], [one.at[1], src(at(-1), 1)])
        self.ring_copy(phase, 5).start()

    def ring_end(self, phase):
        for n in range(2, 6):
            self.ring_copy(phase, n).wait_recv()

    def y_part(self, side):
        m, r0, r, c0, c, order = self.spec
        return self.grads[m].at[:, :, side, pl.ds(r0, r), pl.ds(c0, c)]

    def y_copy(self):
        away = 1 - self.co[2]
        src = self.y_part(away) if self.y_first else self.H.at[:, :, away]
        return self.copy(6, src, self.b["b3"], "y", 0)

    def y_end(self):
        self.y_copy().wait_recv()
        if self.y_first:
            own = self.y_part(self.co[2])
            for i in range(4):
                _add_into(self.K.at[i], [own.at[i], self.K.at[i]])
            return
        for half in (0, 1):
            _add_into(
                self.K.at[half], [self.H.at[half, :, self.co[2]], self.b["b3"].at[half]]
            )

    def first_sum(self):
        self.ring_end(0)
        p = self.ring(0)[1](0)
        two = self.b["b2"]
        for half in (0, 1):
            _add_into(self.H.at[half], [self.g(p, half), two.at[0, half], two.at[1, half]])

    def last_sum(self):
        self.ring_end(1)
        p = self.ring(1)[1](0)
        two = self.b["c2"]
        m, r0, r, c0, c, order = self.spec
        h = c // 2
        for half in (0, 1):
            v = self.kk(p, half)[...].astype(f32) + two[0, half].astype(f32)
            v = v + two[1, half].astype(f32)
            if m == 3:
                self.outs[m][pl.ds(r0, r), c0 // HALF, pl.ds(c0 % HALF + half * h, h)] = v
            else:
                self.outs[m][pl.ds(r0, r), pl.ds(c0 + half * h, h)] = v

    def stage(self, n):
        if self.y_first:
            if n == 0:
                self.y_copy().start()
            elif n == 1:
                self.y_end()
                self.ring_start(0)
            elif n == 2:
                self.ring_mid(0)
            elif n == 3:
                self.first_sum()
                self.ring_start(1)
            elif n == 4:
                self.ring_mid(1)
            else:
                self.last_sum()
        elif n == 0:
            self.ring_start(0)
        elif n == 1:
            self.ring_mid(0)
        elif n == 2:
            self.first_sum()
            self.y_copy().start()
        elif n == 3:
            self.y_end()
            self.ring_start(1)
        elif n == 4:
            self.ring_mid(1)
        else:
            self.last_sum()

    def drain(self):
        for phase in (0, 1):
            for n in range(6):
                self.ring_copy(phase, n).wait_send()
        self.y_copy().wait_send()


def _nn(a, b):
    return lax.dot_general(a, b, (((1,), (0,)), ((), ())), preferred_element_type=f32)


def _nt(a, b):
    return lax.dot_general(a, b, (((1,), (1,)), ((), ())), preferred_element_type=f32)


def _tn(a, b):
    return lax.dot_general(a, b, (((0,), (0,)), ((), ())), preferred_element_type=f32)


def _norm(v):
    centre = v - jnp.mean(v, axis=-1, keepdims=True)
    inv = lax.rsqrt(jnp.mean(centre * centre, axis=-1, keepdims=True) + EPS)
    return centre * inv, inv


def _norm_back(upstream, hat, inv, gain):
    q = upstream * gain
    return inv * (
        q - jnp.mean(q, axis=-1, keepdims=True) - hat * jnp.mean(q * hat, axis=-1, keepdims=True)
    )


def _cols(i, n):
    return pl.ds(pl.multiple_of(i * n, n), n)


def _image_rows(img, body):
    base = img * PAD

    def step(i):
        for part in (0, 32):
            body(pl.ds(pl.multiple_of(base + i * 64 + part, 16), 32))

    _loop(3, step)
    body(pl.ds(base + 192, 16))


def _kernel(*refs):
    (counts, order, images, cotangent, gain_one, gain_two, wqkv_in, wo_in, w1_in, w2_in) = refs[:10]
    (y_ref, ig_ref, o_w2, o_w1, o_wo, o_qkv, o_gain) = refs[10:17]
    rest = refs[17:]
    (
        wqkv, wo, w1, w2, g_w2, g_w1, g_wo, g_qkv, g_gain,
        xb, eb, hin, n1, pr, pb, mx, mid, n2, act, gp, eg, mlow, pg, sendb, recvb, gacc,
        load_sem, x_ss, x_rs, hop_sem, rs_ss, rs_rs,
    ) = rest[:32]
    ring_bufs = rest[32:]

    section = lax.axis_index("section")
    tensor = lax.axis_index("tensor")
    dp = lax.axis_index("dp")
    z, x, y = dp // 8, lax.rem(dp // 2, 4), lax.rem(dp, 2)

    def load(i):
        if i < 3:
            src, dst = wqkv_in.at[i], wqkv.at[:, pl.ds(i * HALF, HALF)]
        else:
            src, dst = ((wo_in, wo), (w1_in, w1), (w2_in, w2))[i - 3]
        return pltpu.make_async_copy(src, dst, load_sem.at[i])

    for i in range(6):
        load(i).start()

    barrier = pltpu.get_barrier_semaphore()

    def r4(v):
        return lax.rem(v + 4, 4)

    for peer in (
        {"tensor": 1 - tensor},
        {"section": 1 - section},
        {"dp": r4(z + 1) * 8 + x * 2 + y},
        {"dp": r4(z - 1) * 8 + x * 2 + y},
        {"dp": z * 8 + r4(x + 1) * 2 + y},
        {"dp": z * 8 + r4(x - 1) * 2 + y},
        {"dp": z * 8 + x * 2 + 1 - y},
    ):
        pl.semaphore_signal(barrier, inc=1, device_id=peer, device_id_type=MESH)

    for img in range(IMGS):
        live = jnp.float32(0)
        for i in range(IMGS):
            held = jnp.where(jnp.logical_and(order[0, i] == img, i < counts[0]), 1.0, 0.0)
            live = live + held
        xb[pl.ds(img * PAD + TOKENS - 5, 16), :] = jnp.zeros((16, D), bf16)
        eb[pl.ds(img * PAD + TOKENS - 5, 16), :] = jnp.zeros((16, D), bf16)
        xb[pl.ds(img * PAD, TOKENS), :] = images[img]
        eb[pl.ds(img * PAD, TOKENS), :] = (cotangent[img].astype(f32) * live).astype(bf16)
    pl.semaphore_wait(barrier, 7)

    def img_rows(img):
        return pl.ds(img * PAD, PAD)

    def exchange(par, img):
        return pltpu.make_async_remote_copy(
            src_ref=sendb.at[par, img_rows(img)],
            dst_ref=recvb.at[par, img_rows(img)],
            send_sem=x_ss.at[par, img],
            recv_sem=x_rs.at[par, img],
            device_id={"tensor": 1 - tensor},
            device_id_type=MESH,
        )

    own_half = pl.ds(pl.multiple_of(tensor * 512, 512), 512)
    other_half = pl.ds(pl.multiple_of((1 - tensor) * 512, 512), 512)

    def hop(src, img):
        return pltpu.make_async_remote_copy(
            src_ref=src.at[img_rows(img), own_half],
            dst_ref=hin.at[img_rows(img), own_half],
            send_sem=hop_sem.at[0, img],
            recv_sem=hop_sem.at[1, img],
            device_id={"section": 1 - section},
            device_id_type=MESH,
        )

    def pass_half(img, cols):
        return pltpu.make_async_remote_copy(
            src_ref=hin.at[img_rows(img), cols],
            dst_ref=hin.at[img_rows(img), cols],
            send_sem=hop_sem.at[2, img],
            recv_sem=hop_sem.at[3, img],
            device_id={"tensor": 1 - tensor},
            device_id_type=MESH,
        )

    def receive(src, dst, img):
        hop(src, img).wait_recv()
        pass_half(img, own_half).start()
        pass_half(img, own_half).wait_send()
        pass_half(img, other_half).wait_recv()
        dst[img_rows(img), :] = hin[img_rows(img), :]

    lane = lax.broadcasted_iota(jnp.int32, (1, 128), 1)
    head_masks = ((lane < 64).astype(bf16), (lane >= 64).astype(bf16))
    key_bias = jnp.where(lax.broadcasted_iota(jnp.int32, (PAD, 1), 0) < TOKENS, 0.0, -1e30)

    def forward(tick):
        first = tick == 0

        @pl.when(jnp.logical_and(tick == 1, section == 0))
        def _():
            for img in (0, 1):
                hop(y_ref, img).wait_send()

        def ln_one(rows):
            hat, inv = _norm(xb[rows, :].astype(f32))
            n1[rows, :] = (hat * gain_one[...]).astype(bf16)

        def project(rows):
            def step(i):
                pr[rows, _cols(i, 512)] = _nn(n1[rows, :], wqkv[:, _cols(i, 512)]).astype(bf16)

            _loop(3, step)

        @pl.when(first)
        def _():
            _image_rows(0, ln_one)
            _image_rows(1, ln_one)
            for i in range(3):
                load(i).wait()
            project(pl.ds(0, ROWS))

        for img in (0, 1):
            @pl.when(tick == 1)
            def _():
                @pl.when(section == 1)
                def _():
                    receive(y_ref, xb, img)

                _image_rows(img, ln_one)
                project(img_rows(img))

            def attend(pair_i):
                rows = img_rows(img)
                q = pr[rows, _cols(pair_i, 128)]
                k = pr[rows, _cols(pair_i + 4, 128)]
                v = pr[rows, _cols(pair_i + 8, 128)]
                total = None
                for h in (0, 1):
                    s = _nt(k, q * (head_masks[h] * 0.125)) + key_bias
                    e = jnp.exp(s - jnp.max(s, axis=0, keepdims=True))
                    p = (e * (1.0 / jnp.sum(e, axis=0, keepdims=True))).astype(bf16)
                    pb[img * 8 + pair_i * 2 + h] = p
                    t = _tn(p, v * head_masks[h])
                    total = t if total is None else total + t
                mx[rows, _cols(pair_i, 128)] = total.astype(bf16)

            _loop(4, attend)

            if img == 0:
                @pl.when(first)
                def _():
                    load(3).wait()

            sendb[0, img_rows(img), :] = _nn(mx[img_rows(img), :], wo[...]).astype(bf16)
            exchange(0, img).start()

        for img in (0, 1):
            exchange(0, img).wait()

            def ln_two(rows):
                m = xb[rows, :].astype(f32) + (
                    sendb[0, rows, :].astype(f32) + recvb[0, rows, :].astype(f32)
                )
                mid[rows, :] = m
                hat, inv = _norm(m)
                n2[rows, :] = (hat * gain_two[...]).astype(bf16)

            _image_rows(img, ln_two)

        @pl.when(first)
        def _():
            load(4).wait()

        def expand(i):
            part = _cols(i, 256)
            e = _nn(n2[...], w1[:, part])
            phi = 0.5 * (1.0 + lax.erf(e * 0.7071067811865476))
            act[:, part] = (e * phi).astype(bf16)
            gp[:, part] = (phi + e * (jnp.exp(-0.5 * e * e) * 0.3989422804014327)).astype(bf16)

        _loop(8, expand)

        @pl.when(first)
        def _():
            load(5).wait()

        for img in (0, 1):
            def reduce(i):
                sendb[1, img_rows(img), _cols(i, 512)] = _nn(
                    act[img_rows(img), :], w2[:, _cols(i, 512)]
                ).astype(bf16)

            _loop(2, reduce)
            exchange(1, img).start()

        for img in (0, 1):
            exchange(1, img).wait()

            def finish(rows):
                v = mid[rows, :] + (sendb[1, rows, :].astype(f32) + recvb[1, rows, :].astype(f32))
                y_ref[rows, :] = v.astype(bf16)

            _image_rows(img, finish)

            @pl.when(jnp.logical_and(first, section == 0))
            def _():
                hop(y_ref, img).start()

    _loop(2, forward)

    grads = (g_w2, g_w1, g_wo, g_qkv, g_gain)
    outs = (o_w2, o_w1, o_wo, o_qkv, o_gain)
    nb = len(BUF_NAMES)
    streams = [
        _Stream(
            i, spec, grads, dict(zip(BUF_NAMES, ring_bufs[i * nb : (i + 1) * nb])), outs,
            (rs_ss, rs_rs), (z, x, y),
        )
        for i, spec in enumerate(STREAMS)
    ]
    groups, count = [], 0
    for g in GROUPS:
        groups.append(streams[count : count + len(g)])
        count += len(g)

    def steps(point):
        for i, stage in STEPS[point]:
            for st in groups[i]:
                st.stage(stage)

    def pack_gain(row, half):
        lanes = lax.broadcasted_iota(jnp.int32, (1024, 128), 0)
        pick = (lax.rem(lanes, 32) == lax.broadcasted_iota(jnp.int32, (1024, 128), 1)).astype(bf16)
        for zz in range(4):
            r = lax.broadcasted_iota(jnp.int32, (128, 1024), 0) // 16 + zz * 8
            c = lax.broadcasted_iota(jnp.int32, (128, 1024), 1) // 32
            spread = jnp.where(r == c, row, 0.0).astype(bf16)
            g_gain[zz, :, :, :, pl.ds(half * 128, 128)] = (
                _nn(spread, pick).astype(bf16).reshape(4, 2, 16, 128)
            )

    def backward(tick):
        last = tick == 1

        def expand_back(rows):
            def step(i):
                part = _cols(i, 256)
                d = _nt(eb[rows, :], w2[part, :])
                eg[rows, part] = (d * gp[rows, part].astype(f32)).astype(bf16)

            _loop(8, step)

        @pl.when(tick == 0)
        def _():
            expand_back(pl.ds(0, ROWS))

        @pl.when(jnp.logical_and(last, section == 1))
        def _():
            for img in (0, 1):
                hop(ig_ref, img).wait_send()

        @pl.when(jnp.logical_and(last, section == 0))
        def _():
            receive(ig_ref, eb, 0)

        @pl.when(last)
        def _():
            expand_back(img_rows(0))

        @pl.when(jnp.logical_and(last, section == 0))
        def _():
            receive(ig_ref, eb, 1)

        @pl.when(last)
        def _():
            def tile(i):
                for n in (0, 1):
                    part = pl.ds(n * 512, 512)
                    t = _tn(act[:, _cols(i, 256)], eb[:, part]).astype(bf16)
                    g_w2[i // 2, pl.ds(lax.rem(i, 2) * 2, 2), :, :, part] = t.reshape(2, 2, 64, 512)

            _loop(8, tile)
            steps("W2")
            expand_back(img_rows(1))
            steps("eb1")

        for img in (0, 1):
            def expand_terms(i):
                sendb[0, img_rows(img), _cols(i, 512)] = _nt(
                    eg[img_rows(img), :], w1[_cols(i, 512), :]
                ).astype(bf16)

            _loop(2, expand_terms)
            exchange(0, img).start()

        @pl.when(last)
        def _():
            def tile(i):
                for n in range(4):
                    part = pl.ds(n * 512, 512)
                    t = _tn(n2[:, _cols(i, 256)], eg[:, part]).astype(bf16)
                    g_w1[i, :, :, :, part] = t.reshape(4, 2, 32, 512)

            steps("et")
            _loop(4, tile)
            steps("W1")

        gacc[...] = jnp.zeros_like(gacc)

        for img in (0, 1):
            exchange(0, img).wait()

            def ln_two_back(rows):
                dn = sendb[0, rows, :].astype(f32) + recvb[0, rows, :].astype(f32)
                hat, inv = _norm(mid[rows, :])
                gacc[0:1, :] += jnp.sum(dn * hat, axis=0, keepdims=True)
                m = eb[rows, :].astype(f32) + _norm_back(dn, hat, inv, gain_two[...])
                mlow[rows, :] = m.astype(bf16)

            _image_rows(img, ln_two_back)

        sendb[1, :, pl.ds(0, HALF)] = _nt(mlow[...], wo[...]).astype(bf16)

        @pl.when(last)
        def _():
            steps("ln2")

            def tile(i):
                for n in (0, 1):
                    part = pl.ds(n * 512, 512)
                    t = _tn(mx[:, _cols(i, 256)], mlow[:, part]).astype(bf16)
                    g_wo[pl.ds(i * 2, 2), :, :, :, part] = t.reshape(2, 4, 2, 16, 512)

            _loop(2, tile)
            steps("Wo")

        def attend_back(img):
            def step(pair_i):
                rows = img_rows(img)
                q = pr[rows, _cols(pair_i, 128)]
                k = pr[rows, _cols(pair_i + 4, 128)]
                v = pr[rows, _cols(pair_i + 8, 128)]
                do = sendb[1, rows, _cols(pair_i, 128)]
                sums = [None, None, None]
                for h in (0, 1):
                    mask = head_masks[h]
                    p = pb[img * 8 + pair_i * 2 + h]
                    pf = p.astype(f32)
                    doh = do * mask
                    dpr = _nt(v, doh)
                    inner = jnp.sum(dpr * pf, axis=0, keepdims=True)
                    ds = (pf * (dpr - inner)).astype(bf16)
                    for j, t in enumerate((_tn(ds, k * mask), _nn(ds, q * mask), _nn(p, doh))):
                        sums[j] = t if sums[j] is None else sums[j] + t
                for j, scale in enumerate((0.125, 0.125, 1.0)):
                    pg[rows, _cols(pair_i + 4 * j, 128)] = (sums[j] * scale).astype(bf16)

            _loop(4, step)

        attend_back(0)

        @pl.when(last)
        def _():
            steps("at0")

        attend_back(1)

        @pl.when(last)
        def _():
            steps("at1")

        for img in (0, 1):
            def input_terms(i):
                sendb[1, img_rows(img), _cols(i, 512)] = _nt(
                    pg[img_rows(img), :], wqkv[_cols(i, 512), :]
                ).astype(bf16)

            _loop(2, input_terms)
            exchange(1, img).start()

        @pl.when(last)
        def _():
            def tile(i):
                for n in range(3):
                    part = pl.ds(n * 512, 512)
                    t = _tn(n1[:, _cols(i, 256)], pg[:, part]).astype(bf16)
                    g_qkv[i, :, :, :, part] = t.reshape(4, 2, 32, 512)

            steps("it")
            _loop(4, tile)
            steps("QKV")

        for img in (0, 1):
            exchange(1, img).wait()

            def ln_one_back(rows):
                dn = sendb[1, rows, :].astype(f32) + recvb[1, rows, :].astype(f32)
                hat, inv = _norm(xb[rows, :].astype(f32))
                gacc[1:2, :] += jnp.sum(dn * hat, axis=0, keepdims=True)
                m = mlow[rows, :].astype(f32) + _norm_back(dn, hat, inv, gain_one[...])
                ig_ref[rows, :] = m.astype(bf16)

            _image_rows(img, ln_one_back)

            @pl.when(jnp.logical_and(tick == 0, section == 1))
            def _():
                hop(ig_ref, img).start()

    _loop(2, backward)
    steps("ln1")
    pack_gain(gacc[1:2, :], 0)
    pack_gain(gacc[0:1, :], 1)
    steps("gain")
    steps("tail")
    for s in streams:
        s.drain()


def _call(*args):
    vmem = pl.BlockSpec(memory_space=pltpu.VMEM)
    hbm = pl.BlockSpec(memory_space=pl.ANY)
    smem = pl.BlockSpec(memory_space=pltpu.SMEM)
    out_shape = [jax.ShapeDtypeStruct((ROWS, D), bf16)] * 2 + [
        jax.ShapeDtypeStruct((32, 3, HALF) if s[1] == QKV else s, f32) for s in GRADS
    ]
    scratch = [
        pltpu.VMEM((D, QKV), bf16),
        pltpu.VMEM((HALF, D), bf16),
        pltpu.VMEM((D, WIDE), bf16),
        pltpu.VMEM((WIDE, D), bf16),
    ]
    scratch += [pltpu.VMEM((4, 4, 2) + s, bf16) for s in GRADS]
    scratch += [
        pltpu.VMEM((ROWS, D), bf16),
        pltpu.VMEM((ROWS, D), bf16),
        pltpu.VMEM((ROWS, D), bf16),
        pltpu.VMEM((ROWS, D), bf16),
        pltpu.VMEM((ROWS, QKV), bf16),
        pltpu.VMEM((16, PAD, PAD), bf16),
        pltpu.VMEM((ROWS, HALF), bf16),
        pltpu.VMEM((ROWS, D), f32),
        pltpu.VMEM((ROWS, D), bf16),
        pltpu.VMEM((ROWS, WIDE), bf16),
        pltpu.VMEM((ROWS, WIDE), bf16),
        pltpu.VMEM((ROWS, WIDE), bf16),
        pltpu.VMEM((ROWS, D), bf16),
        pltpu.VMEM((ROWS, QKV), bf16),
        pltpu.VMEM((2, ROWS, D), bf16),
        pltpu.VMEM((2, ROWS, D), bf16),
        pltpu.VMEM((8, D), f32),
        pltpu.SemaphoreType.DMA((6,)),
        pltpu.SemaphoreType.DMA((2, 2)),
        pltpu.SemaphoreType.DMA((2, 2)),
        pltpu.SemaphoreType.DMA((4, 2)),
        pltpu.SemaphoreType.DMA((len(STREAMS), 13)),
        pltpu.SemaphoreType.DMA((len(STREAMS), 13)),
    ]
    for s in STREAMS:
        scratch += [pltpu.VMEM(b, bf16) for b in _buffers(s)]
    return pl.pallas_call(
        _kernel,
        out_shape=out_shape,
        in_specs=[smem, smem, vmem, vmem, vmem, vmem, hbm, hbm, hbm, hbm],
        out_specs=[vmem] * len(out_shape),
        scratch_shapes=scratch,
        compiler_params=pltpu.CompilerParams(
            collective_id=0, has_side_effects=True, vmem_limit_bytes=63 << 20
        ),
    )(*args)


def per_device(
    images, cotangent, shard_count, slot_order, attend_gain, attend_input, attend_output,
    feed_gain, feed_expand, feed_reduce,
):
    y, ig, d_w2, d_w1, d_wo, d_qkv, d_gain = _call(
        shard_count, slot_order, images[0, :, 0], cotangent[0, :, 0], attend_gain, feed_gain,
        jnp.moveaxis(attend_input[0], 1, 0), attend_output[0], feed_expand[0], feed_reduce[0],
    )

    def cut(v):
        return v.reshape(IMGS, PAD, D)[:, :TOKENS].reshape(1, 1, IMGS, 1, TOKENS, D)

    return (
        cut(y), cut(ig), d_gain[0:1, 0:32], d_qkv[None], d_wo[None],
        d_gain[0:1, 128:160], d_w1[None], d_w2[None],
    )


def solution(mesh):
    in_specs = (
        P("dp", None, None, None, None),
        P("dp", None, None, None, None),
        P("dp"),
        P("dp", None),
        P("section", None),
        P("section", None, None, "tensor"),
        P("section", "tensor", None),
        P("section", None),
        P("section", None, "tensor"),
        P("section", "tensor", None),
    )
    out_specs = (
        P("section", "dp", None, None, None, None),
        P("section", "dp", None, None, None, None),
        P("section", "dp"),
        P("section", "dp", None, "tensor"),
        P("section", ("tensor", "dp"), None),
        P("section", "dp"),
        P("section", "dp", "tensor"),
        P("section", ("tensor", "dp"), None),
    )
    return jax.shard_map(
        per_device, mesh=mesh, in_specs=in_specs, out_specs=out_specs, check_vma=False
    )
```

time: 215 us -> 182 us (0.85)
  Pallas kernels: 193 us -> 168 us
  local copies, waits for them, and re-layouts: 18 us -> 12.9 us
    pallas_call x1, Pallas kernels: 193 us -> 168 us  [_call(): pl.pallas_call(_kernel, out_shape=out_shape, in_specs=[smem, smem, vmem,...]
    squeeze x0 -> x1, local copies, waits for them, and re-layouts: none -> 3.01 us  [per_device(): cotangent[0, :, 0]]
    reshape x2 -> x0, local copies, waits for them, and re-layouts: 2.96 us -> none  [the longest x1 2.82 us: cut(): return v.reshape(IMGS, PAD, D)[:, :TOKENS].reshape(1, 1, IMGS, 1, TOKENS, D)]
    another operation x1 -> x0, local copies, waits for them, and re-layouts: 2.95 us -> none  [per_device(): attend_input[0].reshape(D, QKV)]
    unnamed x19 -> x14, local copies, waits for them, and re-layouts: 6.4 us -> 6.23 us
where the time goes in v2:
time: 182 us
  Pallas kernels  168 us (92%)
  local copies, waits for them, and re-layouts  12.9 us (7%)
    pallas_call x1, Pallas kernels, _call(): pl.pallas_call(_kernel, out_shape=out_shape, in_specs=[smem, smem, vmem,...  168 us
    unnamed x14, local copies, waits for them, and re-layouts  6.23 us

profile of v2, /device:TPU:0, one launch (start us, length us, event | category | flops | bytes accessed | tf_op | source)
XLA Modules:
  0.0 181.8 jit_solution(7946413192214904239)
XLA Ops:
  1.3 3.0 %copy_bitcast_fusion = (bf16[2,197,1024]{2,1,0:T(8,128)(2,1)}, bf16[2,197,1024]{2,1,0:T(8,128)(2,1)}) fusion(bf16[1,2,1,197,1024]{4,1,3,2,0:T(2,128)(2,1)} %param.11, bf16[1,2,1,197,1024]{4,1,3,2,0:T(2,128)(2,1)} %param.10), kind=kLoop, calls=%fused_computation | loop fusion | bytes 3227648 | tf_op jit(solution)/shard_map/squeeze | solution.py:785
  4.3 167.6 %shard_map.161 = (bf16[416,1024]{1,0:T(8,128)(2,1)}, bf16[416,1024]{1,0:T(8,128)(2,1)}, f32[64,1024]{1,0:T(8,128)}, f32[32,2048]{1,0:T(8,128)}, f32[16,1024]{1,0...) custom-call(s32[1]{0:T(128)S(6)} %copy.34.refs_0_, s32[1,2]{1,0:T(1,128)} %refs_1_.1, ...), custom_call_target="tpu_custom_call" | custom-call | tf_op jit(solution)/shard_map/pallas_call | solution.py:768
  171.9 0.0 copy-start
  171.9 0.0 copy-start.3
  171.9 0.0 copy-start.2
  171.9 0.0 copy-start.1
  171.9 1.3 slice.16
  173.2 1.7 copy.30
  174.9 1.2 slice.17
  176.1 1.7 copy.29
  177.8 1.2 fusion
  179.1 0.0 copy-done
  179.1 0.7 copy.22
  179.8 0.0 copy-done.3
  179.8 0.6 copy.35
  180.4 0.0 copy-done.2
  180.4 0.7 copy.36
  181.1 0.0 copy-done.1
  181.1 0.7 copy.37
Async XLA Ops:
  171.9 7.2 %copy-start = (f32[32,3,512]{2,1,0:T(4,128)S(1)}, f32[32,3,512]{2,1,0:T(4,128)}, u32[]{:S(2)}) copy-start(f32[32,3,512]{2,1,0:T(4,128)} %get-tuple-element.18) | copy-start | bytes 589828
  171.9 7.9 %copy-start.3 = (f32[16,1024]{1,0:T(8,128)S(1)}, f32[16,1024]{1,0:T(8,128)}, u32[]{:S(2)}) copy-start(f32[16,1024]{1,0:T(8,128)} %get-tuple-element.19) | copy-start | bytes 196612
  171.9 8.5 %copy-start.2 = (f32[32,2048]{1,0:T(8,128)S(1)}, f32[32,2048]{1,0:T(8,128)}, u32[]{:S(2)}) copy-start(f32[32,2048]{1,0:T(8,128)} %get-tuple-element.20) | copy-start | bytes 786436
  171.9 9.2 %copy-start.1 = (f32[64,1024]{1,0:T(8,128)S(1)}, f32[64,1024]{1,0:T(8,128)}, u32[]{:S(2)}) copy-start(f32[64,1024]{1,0:T(8,128)} %get-tuple-element.21) | copy-start | bytes 786436

commit v3 on v2

--- a/solution.py
+++ b/solution.py
@@ -32,8 +32,8 @@
     def pair(m, r0, r, c0, c, order=0):
         groups.append(((m, r0, r, c0, c // 2, order), (m, r0, r, c0 + c // 2, c // 2, order + 1)))
 
-    pair(0, 0, 32, 0, 1024)
-    pair(0, 32, 32, 0, 1024, 2)
+    pair(0, 0, 64, 0, 512)
+    pair(0, 0, 64, 512, 512, 2)
     pair(1, 0, 32, 0, 1024)
     pair(1, 0, 32, 1024, 1024)
     pair(2, 0, 16, 0, 1024)
@@ -52,14 +52,14 @@
     "et": ((0, 1),),
     "W1": ((2, 0), (3, 0)),
     "ln2": ((0, 2),),
-    "Wo": ((4, 0),),
+    "Wo": (),
     "at0": ((2, 1),),
-    "at1": (),
+    "at1": ((4, 0),),
     "it": ((3, 1),),
-    "QKV": ((4, 1), (5, 0)),
-    "ln1": ((1, 1),),
-    "gain": (),
-    "tail": ((6, 0), (2, 2), (7, 0), (0, 3), (3, 2), (4, 2), (5, 1), (8, 0), (2, 3), (1, 2), (6, 1), (3, 3), (7, 1), (0, 4), (4, 3), (5, 2), (8, 1), (2, 4), (1, 3), (6, 2), (3, 4), (5, 3), (7, 2), (0, 5), (4, 4), (8, 2), (2, 5), (1, 4), (3, 5), (5, 4), (6, 3), (4, 5), (1, 5), (5, 5), (6, 4), (7, 3), (8, 3), (6, 5), (7, 4), (8, 4), (7, 5), (8, 5)),
+    "QKV": ((5, 0),),
+    "ln1": ((6, 0), (1, 1), (2, 2)),
+    "gain": ((4, 1),),
+    "tail": ((0, 3), (3, 2), (5, 1), (7, 0), (6, 1), (2, 3), (1, 2), (8, 0), (4, 2), (0, 4), (3, 3), (5, 2), (7, 1), (4, 3), (6, 2), (2, 4), (5, 3), (1, 3), (8, 1), (0, 5), (3, 4), (6, 3), (7, 2), (4, 4), (2, 5), (5, 4), (1, 4), (8, 2), (3, 5), (6, 4), (4, 5), (5, 5), (1, 5), (7, 3), (6, 5), (8, 3), (7, 4), (8, 4), (7, 5), (8, 5)),
 }
 STREAMS = [s for g in GROUPS for s in g]
 BUF_NAMES = ("b1", "b2", "b3", "c1", "c2")
@@ -452,7 +452,8 @@
                     total = t if total is None else total + t
                 mx[rows, _cols(pair_i, 128)] = total.astype(bf16)
 
-            _loop(4, attend)
+            for pair_static in range(4):
+                attend(pair_static)
 
             if img == 0:
                 @pl.when(first)
@@ -582,10 +583,8 @@
         @pl.when(last)
         def _():
             def tile(i):
-                for n in (0, 1):
-                    part = pl.ds(n * 512, 512)
-                    t = _tn(act[:, _cols(i, 256)], eb[:, part]).astype(bf16)
-                    g_w2[i // 2, pl.ds(lax.rem(i, 2) * 2, 2), :, :, part] = t.reshape(2, 2, 64, 512)
+                t = _tn(act[:, _cols(i, 256)], eb[...]).astype(bf16)
+                g_w2[i // 2, pl.ds(lax.rem(i, 2) * 2, 2)] = t.reshape(2, 2, 64, D)
 
             _loop(8, tile)
             steps("W2")
@@ -604,10 +603,10 @@
         @pl.when(last)
         def _():
             def tile(i):
-                for n in range(4):
-                    part = pl.ds(n * 512, 512)
+                for n in (0, 1):
+                    part = pl.ds(n * 1024, 1024)
                     t = _tn(n2[:, _cols(i, 256)], eg[:, part]).astype(bf16)
-                    g_w1[i, :, :, :, part] = t.reshape(4, 2, 32, 512)
+                    g_w1[i, :, :, :, part] = t.reshape(4, 2, 32, 1024)
 
             steps("et")
             _loop(4, tile)
@@ -663,7 +662,8 @@
                 for j, scale in enumerate((0.125, 0.125, 1.0)):
                     pg[rows, _cols(pair_i + 4 * j, 128)] = (sums[j] * scale).astype(bf16)
 
-            _loop(4, step)
+            for pair_static in range(4):
+                step(pair_static)
 
         attend_back(0)
 
@@ -689,10 +689,8 @@
         @pl.when(last)
         def _():
             def tile(i):
-                for n in range(3):
-                    part = pl.ds(n * 512, 512)
-                    t = _tn(n1[:, _cols(i, 256)], pg[:, part]).astype(bf16)
-                    g_qkv[i, :, :, :, part] = t.reshape(4, 2, 32, 512)
+                t = _tn(n1[:, _cols(i, 256)], pg[...]).astype(bf16)
+                g_qkv[i] = t.reshape(4, 2, 32, QKV)
 
             steps("it")
             _loop(4, tile)

time: 182 us -> 173 us (0.951)
  Pallas kernels: 168 us -> 159 us
    pallas_call x1, Pallas kernels: 168 us -> 159 us  [_call(): pl.pallas_call(_kernel, out_shape=out_shape, in_specs=[smem, smem, vmem,...]
where the time goes in v3:
time: 173 us
  Pallas kernels  159 us (92%)
  local copies, waits for them, and re-layouts  12.9 us (7%)
    pallas_call x1, Pallas kernels, _call(): pl.pallas_call(_kernel, out_shape=out_shape, in_specs=[smem, smem, vmem,...  159 us
    unnamed x14, local copies, waits for them, and re-layouts  6.23 us

profile of v3, /device:TPU:0, one launch (start us, length us, event | category | flops | bytes accessed | tf_op | source)
XLA Modules:
  0.0 173.0 jit_solution(10420655600420132656)
XLA Ops:
  1.3 3.0 %copy_bitcast_fusion = (bf16[2,197,1024]{2,1,0:T(8,128)(2,1)}, bf16[2,197,1024]{2,1,0:T(8,128)(2,1)}) fusion(bf16[1,2,1,197,1024]{4,1,3,2,0:T(2,128)(2,1)} %param.11, bf16[1,2,1,197,1024]{4,1,3,2,0:T(2,128)(2,1)} %param.10), kind=kLoop, calls=%fused_computation | loop fusion | bytes 3227648 | tf_op jit(solution)/shard_map/squeeze | solution.py:783
  4.3 158.8 %shard_map.161 = (bf16[416,1024]{1,0:T(8,128)(2,1)}, bf16[416,1024]{1,0:T(8,128)(2,1)}, f32[64,1024]{1,0:T(8,128)}, f32[32,2048]{1,0:T(8,128)}, f32[16,1024]{1,0...) custom-call(s32[1]{0:T(128)S(6)} %copy.34.refs_0_, s32[1,2]{1,0:T(1,128)} %refs_1_.1, ...), custom_call_target="tpu_custom_call" | custom-call | tf_op jit(solution)/shard_map/pallas_call | solution.py:766
  163.1 0.0 copy-start
  163.1 0.0 copy-start.3
  163.1 0.0 copy-start.2
  163.1 0.0 copy-start.1
  163.1 1.3 slice.16
  164.4 1.7 copy.30
  166.1 1.2 slice.17
  167.3 1.7 copy.29
  169.0 1.2 fusion
  170.2 0.0 copy-done
  170.2 0.7 copy.22
  171.0 0.0 copy-done.3
  171.0 0.6 copy.35
  171.6 0.0 copy-done.2
  171.6 0.7 copy.36
  172.3 0.0 copy-done.1
  172.3 0.7 copy.37
Async XLA Ops:
  163.1 7.2 %copy-start = (f32[32,3,512]{2,1,0:T(4,128)S(1)}, f32[32,3,512]{2,1,0:T(4,128)}, u32[]{:S(2)}) copy-start(f32[32,3,512]{2,1,0:T(4,128)} %get-tuple-element.18) | copy-start | bytes 589828
  163.1 7.9 %copy-start.3 = (f32[16,1024]{1,0:T(8,128)S(1)}, f32[16,1024]{1,0:T(8,128)}, u32[]{:S(2)}) copy-start(f32[16,1024]{1,0:T(8,128)} %get-tuple-element.19) | copy-start | bytes 196612
  163.1 8.5 %copy-start.2 = (f32[32,2048]{1,0:T(8,128)S(1)}, f32[32,2048]{1,0:T(8,128)}, u32[]{:S(2)}) copy-start(f32[32,2048]{1,0:T(8,128)} %get-tuple-element.20) | copy-start | bytes 786436
  163.1 9.2 %copy-start.1 = (f32[64,1024]{1,0:T(8,128)S(1)}, f32[64,1024]{1,0:T(8,128)}, u32[]{:S(2)}) copy-start(f32[64,1024]{1,0:T(8,128)} %get-tuple-element.21) | copy-start | bytes 786436

commit v4 on v3

--- a/solution.py
+++ b/solution.py
@@ -84,6 +84,14 @@
         return c
 
     lax.fori_loop(0, n, step, 0)
+
+
+def _loop2(n, body):
+    def two(i):
+        body(2 * i)
+        body(2 * i + 1)
+
+    _loop(n // 2, two)
 
 
 def _add_into(dst, srcs):
@@ -352,7 +360,6 @@
         eb[pl.ds(img * PAD + TOKENS - 5, 16), :] = jnp.zeros((16, D), bf16)
         xb[pl.ds(img * PAD, TOKENS), :] = images[img]
         eb[pl.ds(img * PAD, TOKENS), :] = (cotangent[img].astype(f32) * live).astype(bf16)
-    pl.semaphore_wait(barrier, 7)
 
     def img_rows(img):
         return pl.ds(img * PAD, PAD)
@@ -401,6 +408,23 @@
     head_masks = ((lane < 64).astype(bf16), (lane >= 64).astype(bf16))
     key_bias = jnp.where(lax.broadcasted_iota(jnp.int32, (PAD, 1), 0) < TOKENS, 0.0, -1e30)
 
+    def ln_one(rows):
+        hat, inv = _norm(xb[rows, :].astype(f32))
+        n1[rows, :] = (hat * gain_one[...]).astype(bf16)
+
+    def project(rows):
+        def step(i):
+            pr[rows, _cols(i, 512)] = _nn(n1[rows, :], wqkv[:, _cols(i, 512)]).astype(bf16)
+
+        _loop(3, step)
+
+    _image_rows(0, ln_one)
+    _image_rows(1, ln_one)
+    for i in range(3):
+        load(i).wait()
+    project(pl.ds(0, ROWS))
+    pl.semaphore_wait(barrier, 7)
+
     def forward(tick):
         first = tick == 0
 
@@ -408,24 +432,6 @@
         def _():
             for img in (0, 1):
                 hop(y_ref, img).wait_send()
-
-        def ln_one(rows):
-            hat, inv = _norm(xb[rows, :].astype(f32))
-            n1[rows, :] = (hat * gain_one[...]).astype(bf16)
-
-        def project(rows):
-            def step(i):
-                pr[rows, _cols(i, 512)] = _nn(n1[rows, :], wqkv[:, _cols(i, 512)]).astype(bf16)
-
-            _loop(3, step)
-
-        @pl.when(first)
-        def _():
-            _image_rows(0, ln_one)
-            _image_rows(1, ln_one)
-            for i in range(3):
-                load(i).wait()
-            project(pl.ds(0, ROWS))
 
         for img in (0, 1):
             @pl.when(tick == 1)
@@ -557,7 +563,7 @@
                 d = _nt(eb[rows, :], w2[part, :])
                 eg[rows, part] = (d * gp[rows, part].astype(f32)).astype(bf16)
 
-            _loop(8, step)
+            _loop2(8, step)
 
         @pl.when(tick == 0)
         def _():

time: 173 us -> 169 us (0.977)
  Pallas kernels: 159 us -> 155 us
    pallas_call x1, Pallas kernels: 159 us -> 155 us  [_call(): pl.pallas_call(_kernel, out_shape=out_shape, in_specs=[smem, smem, vmem,...]
where the time goes in v4:
time: 169 us
  Pallas kernels  155 us (92%)
  local copies, waits for them, and re-layouts  12.9 us (8%)
    pallas_call x1, Pallas kernels, _call(): pl.pallas_call(_kernel, out_shape=out_shape, in_specs=[smem, smem, vmem,...  155 us
    unnamed x14, local copies, waits for them, and re-layouts  6.23 us

profile of v4, /device:TPU:0, one launch (start us, length us, event | category | flops | bytes accessed | tf_op | source)
XLA Modules:
  0.0 168.8 jit_solution(11698601394471119897)
XLA Ops:
  1.3 3.0 %copy_bitcast_fusion = (bf16[2,197,1024]{2,1,0:T(8,128)(2,1)}, bf16[2,197,1024]{2,1,0:T(8,128)(2,1)}) fusion(bf16[1,2,1,197,1024]{4,1,3,2,0:T(2,128)(2,1)} %param.11, bf16[1,2,1,197,1024]{4,1,3,2,0:T(2,128)(2,1)} %param.10), kind=kLoop, calls=%fused_computation | loop fusion | bytes 3227648 | tf_op jit(solution)/shard_map/squeeze | solution.py:789
  4.3 154.6 %shard_map.161 = (bf16[416,1024]{1,0:T(8,128)(2,1)}, bf16[416,1024]{1,0:T(8,128)(2,1)}, f32[64,1024]{1,0:T(8,128)}, f32[32,2048]{1,0:T(8,128)}, f32[16,1024]{1,0...) custom-call(s32[1]{0:T(128)S(6)} %copy.34.refs_0_, s32[1,2]{1,0:T(1,128)} %refs_1_.1, ...), custom_call_target="tpu_custom_call" | custom-call | tf_op jit(solution)/shard_map/pallas_call | solution.py:772
  158.9 0.0 copy-start
  158.9 0.0 copy-start.3
  158.9 0.0 copy-start.2
  158.9 0.0 copy-start.1
  158.9 1.3 slice.16
  160.2 1.7 %copy.30 = bf16[2,197,1024]{2,0,1:T(2,128)(2,1)} copy(bf16[2,197,1024]{2,1,0:T(8,128)(2,1)S(1)} %slice.16) | data formatting | bytes 1613824
  161.9 1.2 slice.17
  163.1 1.7 %copy.29 = bf16[2,197,1024]{2,0,1:T(2,128)(2,1)} copy(bf16[2,197,1024]{2,1,0:T(8,128)(2,1)S(1)} %slice.17) | data formatting | bytes 1613824
  164.8 1.2 fusion
  166.0 0.0 copy-done
  166.0 0.7 copy.22
  166.8 0.0 copy-done.3
  166.8 0.6 copy.35
  167.4 0.0 copy-done.2
  167.4 0.7 copy.36
  168.1 0.0 copy-done.1
  168.1 0.7 copy.37
Async XLA Ops:
  158.9 7.2 %copy-start = (f32[32,3,512]{2,1,0:T(4,128)S(1)}, f32[32,3,512]{2,1,0:T(4,128)}, u32[]{:S(2)}) copy-start(f32[32,3,512]{2,1,0:T(4,128)} %get-tuple-element.18) | copy-start | bytes 589828
  158.9 7.9 %copy-start.3 = (f32[16,1024]{1,0:T(8,128)S(1)}, f32[16,1024]{1,0:T(8,128)}, u32[]{:S(2)}) copy-start(f32[16,1024]{1,0:T(8,128)} %get-tuple-element.19) | copy-start | bytes 196612
  158.9 8.5 %copy-start.2 = (f32[32,2048]{1,0:T(8,128)S(1)}, f32[32,2048]{1,0:T(8,128)}, u32[]{:S(2)}) copy-start(f32[32,2048]{1,0:T(8,128)} %get-tuple-element.20) | copy-start | bytes 786436
  158.9 9.2 %copy-start.1 = (f32[64,1024]{1,0:T(8,128)S(1)}, f32[64,1024]{1,0:T(8,128)}, u32[]{:S(2)}) copy-start(f32[64,1024]{1,0:T(8,128)} %get-tuple-element.21) | copy-start | bytes 786436

commit v5 on v4

--- a/solution.py
+++ b/solution.py
@@ -493,7 +493,7 @@
             act[:, part] = (e * phi).astype(bf16)
             gp[:, part] = (phi + e * (jnp.exp(-0.5 * e * e) * 0.3989422804014327)).astype(bf16)
 
-        _loop(8, expand)
+        _loop2(8, expand)
 
         @pl.when(first)
         def _():

time: 169 us -> 169 us (level)
  no operation moved by 1% of the time
where the time goes in v5:
time: 169 us; the launch traced here: 168 us
  Pallas kernels  154 us (91%)
  local copies, waits for them, and re-layouts  12.9 us (8%)
    pallas_call x1, Pallas kernels, _call(): pl.pallas_call(_kernel, out_shape=out_shape, in_specs=[smem, smem, vmem,...  154 us
    unnamed x14, local copies, waits for them, and re-layouts  6.23 us

profile of v5, /device:TPU:0, one launch (start us, length us, event | category | flops | bytes accessed | tf_op | source)
XLA Modules:
  0.0 168.4 jit_solution(3585207688292088872)
XLA Ops:
  1.3 3.0 %copy_bitcast_fusion = (bf16[2,197,1024]{2,1,0:T(8,128)(2,1)}, bf16[2,197,1024]{2,1,0:T(8,128)(2,1)}) fusion(bf16[1,2,1,197,1024]{4,1,3,2,0:T(2,128)(2,1)} %param.11, bf16[1,2,1,197,1024]{4,1,3,2,0:T(2,128)(2,1)} %param.10), kind=kLoop, calls=%fused_computation | loop fusion | bytes 3227648 | tf_op jit(solution)/shard_map/squeeze | solution.py:789
  4.3 154.1 %shard_map.161 = (bf16[416,1024]{1,0:T(8,128)(2,1)}, bf16[416,1024]{1,0:T(8,128)(2,1)}, f32[64,1024]{1,0:T(8,128)}, f32[32,2048]{1,0:T(8,128)}, f32[16,1024]{1,0...) custom-call(s32[1]{0:T(128)S(6)} %copy.34.refs_0_, s32[1,2]{1,0:T(1,128)} %refs_1_.1, ...), custom_call_target="tpu_custom_call" | custom-call | tf_op jit(solution)/shard_map/pallas_call | solution.py:772
  158.4 0.0 copy-start
  158.4 0.0 copy-start.3
  158.4 0.0 copy-start.2
  158.5 0.0 copy-start.1
  158.5 1.3 slice.16
  159.7 1.7 %copy.30 = bf16[2,197,1024]{2,0,1:T(2,128)(2,1)} copy(bf16[2,197,1024]{2,1,0:T(8,128)(2,1)S(1)} %slice.16) | data formatting | bytes 1613824
  161.5 1.2 slice.17
  162.7 1.7 %copy.29 = bf16[2,197,1024]{2,0,1:T(2,128)(2,1)} copy(bf16[2,197,1024]{2,1,0:T(8,128)(2,1)S(1)} %slice.17) | data formatting | bytes 1613824
  164.4 1.2 fusion
  165.6 0.0 copy-done
  165.6 0.7 copy.22
  166.3 0.0 copy-done.3
  166.3 0.6 copy.35
  167.0 0.0 copy-done.2
  167.0 0.7 copy.36
  167.7 0.0 copy-done.1
  167.7 0.7 copy.37
Async XLA Ops:
  158.4 7.2 %copy-start = (f32[32,3,512]{2,1,0:T(4,128)S(1)}, f32[32,3,512]{2,1,0:T(4,128)}, u32[]{:S(2)}) copy-start(f32[32,3,512]{2,1,0:T(4,128)} %get-tuple-element.18) | copy-start | bytes 589828
  158.4 7.9 %copy-start.3 = (f32[16,1024]{1,0:T(8,128)S(1)}, f32[16,1024]{1,0:T(8,128)}, u32[]{:S(2)}) copy-start(f32[16,1024]{1,0:T(8,128)} %get-tuple-element.19) | copy-start | bytes 196612
  158.4 8.5 %copy-start.2 = (f32[32,2048]{1,0:T(8,128)S(1)}, f32[32,2048]{1,0:T(8,128)}, u32[]{:S(2)}) copy-start(f32[32,2048]{1,0:T(8,128)} %get-tuple-element.20) | copy-start | bytes 786436
  158.5 9.2 %copy-start.1 = (f32[64,1024]{1,0:T(8,128)S(1)}, f32[64,1024]{1,0:T(8,128)}, u32[]{:S(2)}) copy-start(f32[64,1024]{1,0:T(8,128)} %get-tuple-element.21) | copy-start | bytes 786436
